TPU v7x, 512 devices: a whole 4x8x8 slice. The times are simulated.
512 devices in a mesh: sub: 64 (over z, y), own: 8 (over x, core).
Axes of the slice: x: 4, y: 8, z: 8, core: 2. Of those that a mesh axis runs over, the one named last changes fastest.
Arguments:
- deflation: float32 [30, 4096, 2048], P(None, 'sub', 'own'), may hold values from -164 to 164
- permeability_base: float32 [4096, 2048], P('sub', 'own'), may hold values from 0.5 to 2
- design_mask: int32 [4096, 2048], P('sub', 'own'), may hold values 0 or 1
- storage: float32 [4096, 2048], P('sub', 'own'), may hold values from 0.0002 to 0.0008
- right_side: float32 [4096, 2048], P('sub', 'own'), may hold values from -4.1 to 4.9
Outputs:
- coarse_coeffs: float32 [64, 30], P('sub')
- new_residual: float32 [4096, 2048], P('sub', 'own')
All inputs are finite; a program needn't handle non-finite values. No bound on the sum of `design_mask` on one device may be relied on, other than what follows from the above.
Results may differ from a plain program's by a relative error of at most 0.00045.
Values sent between devices are 32-bit elements; how exact they have to be, the bound alone decides.
No kernel may reach another device: no remote copies, remote signals or barrier semaphores. Data moves between devices by JAX's collectives and lax.ppermute only.
A program may use at most 128 MiB of HBM per device.

v0:
```python
import functools
import math

import jax
import jax.numpy as jnp
from jax import lax
from jax.experimental import pallas as pl
from jax.experimental.pallas import tpu as pltpu
from jax.sharding import PartitionSpec as P

LOG_CONTRAST = math.log(1000.0)
precise = lax.Precision.HIGHEST
NV = 30
NT = (((1,), (1,)), ((), ()))
VMEM = pl.BlockSpec(memory_space=pltpu.VMEM)
SMEM = pl.BlockSpec(memory_space=pltpu.SMEM)


def f32(*shape):
    return jax.ShapeDtypeStruct(shape, jnp.float32)


def limit(mib):
    return pltpu.CompilerParams(vmem_limit_bytes=mib * 1024 * 1024)


def iota(shape, dim):
    return lax.broadcasted_iota(jnp.int32, shape, dim)


def transmit(centre, beside):
    return 2.0 * centre * beside / (centre + beside)


def split_parts(x):
    high = x.astype(jnp.bfloat16)
    rest = x - high.astype(jnp.float32)
    middle = rest.astype(jnp.bfloat16)
    low = (rest - middle.astype(jnp.float32)).astype(jnp.bfloat16)
    return high, middle, low


def edges_kernel(z_ref, base_ref, mask_ref, k_ref, first_ref, last_ref, head, tail, sems):
    nx = z_ref.shape[1]
    vectors = z_ref.shape[0]
    copies = [
        pltpu.make_async_copy(z_ref.at[:, pl.ds(0, 8), :], head, sems.at[0]),
        pltpu.make_async_copy(z_ref.at[:, pl.ds(nx - 8, 8), :], tail, sems.at[1]),
    ]
    for c in copies:
        c.start()
    k = base_ref[...] * jnp.exp((mask_ref[...].astype(jnp.float32) - 1.0) * LOG_CONTRAST)
    k_ref[...] = k
    for c in copies:
        c.wait()
    ny = k.shape[1]
    pad = jnp.zeros((31 - vectors, ny), jnp.float32)
    first_ref[...] = jnp.concatenate([head[v, 0:1, :] for v in range(vectors)] + [k[0:1]] + [pad], 0)
    last_ref[...] = jnp.concatenate([tail[v, 7:8, :] for v in range(vectors)] + [k[nx - 1 : nx]] + [pad], 0)


def edges(z, base, mask):
    vectors, nx, ny = z.shape
    return pl.pallas_call(
        edges_kernel,
        out_shape=[f32(nx, ny), f32(32, ny), f32(32, ny)],
        in_specs=[pl.BlockSpec(memory_space=pl.ANY), VMEM, VMEM],
        out_specs=[VMEM, VMEM, VMEM],
        scratch_shapes=[
            pltpu.VMEM((vectors, 8, ny), jnp.float32),
            pltpu.VMEM((vectors, 8, ny), jnp.float32),
            pltpu.SemaphoreType.DMA((2,)),
        ],
        name="edges",
    )(z, base, mask)


def assemble_kernel(z_ref, k_ref, st_ref, rs_ref, p_ref, c_ref, az_ref):
    vectors, nx, ny = z_ref.shape
    k = k_ref[...]
    st = st_ref[...]
    row, lane = iota((nx, ny), 0), iota((nx, ny), 1)
    tn = jnp.where(lane == ny - 1, 0.0, transmit(k, pltpu.roll(k, ny - 1, 1)))
    te = jnp.where(row == nx - 1, 0.0, transmit(k, pltpu.roll(k, nx - 1, 0)))

    def apply(v, _):
        z = z_ref[v]
        fn = tn * (pltpu.roll(z, ny - 1, 1) - z)
        fe = te * (pltpu.roll(z, nx - 1, 0) - z)
        az_ref[v] = st * z - fn + pltpu.roll(fn, 1, 1) - fe + pltpu.roll(fe, 1, 0)
        return 0

    lax.fori_loop(0, vectors, apply, 0, unroll=2)
    az_ref[vectors] = rs_ref[...]
    az_ref[vectors + 1] = jnp.zeros((nx, ny), jnp.float32)

    groups = nx // 8
    pick_n, pick_c = iota((128, ny), 0), iota((128, ny), 1)
    edge_lane = jnp.where(((pick_n >> 3) & 1) == 0, 0, ny - 1)
    gram, columns = None, None
    for g in range(groups):
        rows = pl.ds(8 * g, 8)
        zg = jnp.concatenate(
            [z_ref[:, rows, :].reshape(8 * vectors, ny), k[8 * g : 8 * g + 8], jnp.zeros((8, ny), jnp.float32)], 0
        )
        ag = az_ref[:, rows, :].reshape(8 * (vectors + 2), ny)
        zh, zm, zl = split_parts(zg)
        ah, am, al = split_parts(ag)
        left = jnp.concatenate([zh, zh, zm, zm, zh, zl], 1)
        right = jnp.concatenate([ah, am, ah, am, al, ah], 1)
        part = lax.dot_general(left, right, NT, preferred_element_type=jnp.float32)
        pick = ((pick_n & 7) == g) & (pick_c == edge_lane)
        pick = pick.astype(jnp.float32).astype(jnp.bfloat16)
        col = lax.dot_general(
            jnp.concatenate([zh, zm, zl], 1), jnp.concatenate([pick] * 3, 1), NT, preferred_element_type=jnp.float32
        )
        gram = part if gram is None else gram + part
        columns = col if columns is None else columns + col
    size = 8 * (vectors + 2)
    same = (iota((size, size), 0) & 7) == (iota((size, size), 1) & 7)
    gram = jnp.where(same, gram, 0.0)
    columns = jnp.where((iota((size, 128), 0) & 7) == (iota((size, 128), 1) >> 4), columns, 0.0)
    fold = (iota((32, size), 0) == (iota((32, size), 1) >> 3)).astype(jnp.float32)
    unfold = (iota((size, 128), 1) == (iota((size, 128), 0) >> 3)).astype(jnp.float32)
    folded = jnp.dot(fold, jnp.concatenate([gram, columns], 1), precision=precise, preferred_element_type=jnp.float32)
    p = jnp.dot(folded[:, :size], unfold, precision=precise, preferred_element_type=jnp.float32)
    p_ref[...] = jnp.where(iota((32, 128), 0) < vectors, p, 0.0)
    c_ref[...] = folded[:, size:]


def assemble(z, k, st, rs):
    vectors, nx, ny = z.shape
    return pl.pallas_call(
        assemble_kernel,
        out_shape=[f32(32, 128), f32(32, 128)],
        in_specs=[VMEM] * 4,
        out_specs=[VMEM, VMEM],
        scratch_shapes=[pltpu.VMEM((vectors + 2, nx, ny), jnp.float32)],
        compiler_params=limit(32),
        cost_estimate=pl.CostEstimate(flops=6 * 2 * 256 * 256 * 256 * 8, bytes_accessed=2 * 1024 * 1024, transcendentals=0),
        name="assemble",
    )(z, k, st, rs)


def pack(tile):
    lane = iota((16, 128), 1)
    return jnp.where(lane < 64, tile[:16], pltpu.roll(tile[16:], 64, 1))


def rim_kernel(first_ref, last_ref, up_ref, down_ref, p_ref, c_ref, out_ref):
    ny = first_ref.shape[1]
    body = iota((32, ny), 0) < NV
    tw = transmit(first_ref[NV : NV + 1], up_ref[NV : NV + 1])
    te = transmit(last_ref[NV : NV + 1], down_ref[NV : NV + 1])
    first = jnp.where(body, first_ref[...], 0.0)
    last = jnp.where(body, last_ref[...], 0.0)
    above = jnp.where(body, up_ref[...], 0.0)
    blank = jnp.zeros((32, ny), jnp.float32)
    left = jnp.concatenate([first * tw, last * te], 1)
    right = jnp.concatenate(
        [jnp.concatenate([first, last], 1), jnp.concatenate([-above, blank], 1), jnp.zeros((64, 2 * ny), jnp.float32)], 0
    )
    both = lax.dot_general(left, right, NT, precision=precise, preferred_element_type=jnp.float32)
    share = jnp.concatenate([pack(p_ref[...] + both), c_ref[...]], 0)
    for o in range(out_ref.shape[0]):
        out_ref[o] = share


def rim(first, last, up, down, p, c, copies):
    return pl.pallas_call(
        rim_kernel,
        out_shape=f32(copies, 48, 128),
        in_specs=[VMEM] * 6,
        out_specs=VMEM,
        name="rim",
    )(first, last, up, down, p, c)


def total_kernel(g_ref, out_ref):
    count = g_ref.shape[0]
    tile = g_ref[0, :16, :]
    for o in range(1, count):
        tile = tile + g_ref[o, :16, :]
    lane = iota((32, 128), 1)
    used = (((lane >> 3) & 1) == 0) & (iota((32, 128), 0) < NV)
    steps, flows = [], []
    for o in range(count - 1):
        here = pltpu.roll(g_ref[o, 16:48, :], 120, 1)
        there = g_ref[o + 1, 16:48, :]
        t = transmit(here[NV : NV + 1], there[NV : NV + 1])
        step = jnp.where(used, there - here, 0.0)
        steps.append(step)
        flows.append(jnp.where(used, t * step, 0.0))
    if steps:
        right = jnp.concatenate([jnp.concatenate(steps, 1), jnp.zeros((96, 128 * len(steps)), jnp.float32)], 0)
        faces = lax.dot_general(
            jnp.concatenate(flows, 1), right, NT, precision=precise, preferred_element_type=jnp.float32
        )
        tile = tile + pack(faces)
    for s in range(out_ref.shape[0]):
        out_ref[s] = tile


def total(g, copies):
    return pl.pallas_call(
        total_kernel,
        out_shape=f32(copies, 16, 128),
        in_specs=[VMEM],
        out_specs=VMEM,
        name="total",
    )(g)


def reciprocal(x):
    r = pl.reciprocal(x, approx=True)
    r = r * (2.0 - x * r)
    return r * (2.0 - x * r)


def small_inverse(p):
    a00, a01, a11 = p[0, 0], p[0, 1], p[1, 1]
    b02, b03, b12, b13 = p[0, 2], p[0, 3], p[1, 2], p[1, 3]
    ia = reciprocal(a00 * a11 - a01 * a01)
    h00, h01, h11 = a11 * ia, a01 * ia, a00 * ia
    w02, w03 = h00 * b02 - h01 * b12, h00 * b03 - h01 * b13
    w12, w13 = h11 * b12 - h01 * b02, h11 * b13 - h01 * b03
    s22 = p[2, 2] - (b02 * w02 + b12 * w12)
    s23 = p[2, 3] - (b02 * w03 + b12 * w13)
    s33 = p[3, 3] - (b03 * w03 + b13 * w13)
    iz = reciprocal(s22 * s33 - s23 * s23)
    i22, i23, i33 = s33 * iz, -(s23 * iz), s22 * iz
    i02, i03 = -(w02 * i22 + w03 * i23), -(w02 * i23 + w03 * i33)
    i12, i13 = -(w12 * i22 + w13 * i23), -(w12 * i23 + w13 * i33)
    i00 = h00 - (w02 * i02 + w03 * i03)
    i01 = -h01 - (w02 * i12 + w03 * i13)
    i11 = h11 - (w12 * i12 + w13 * i13)
    return [[i00, i01, i02, i03], [i01, i11, i12, i13], [i02, i12, i22, i23], [i03, i13, i23, i33]]


def take(x, index):
    return jnp.take_along_axis(x, index, axis=1)


def invert_packed(arrays):
    lanes = lax.broadcasted_iota(jnp.int32, (8, 128), 1)
    rows = lax.broadcasted_iota(jnp.int32, (8, 128), 0)
    start, inner = lanes & ~31, lanes & 31
    for k in range(0, 32, 4):
        index = [start + (k + b) for b in range(4)]
        inside = (inner >= k) & (inner < k + 4)
        tile = k // 8
        out = []
        for a in arrays:
            tiles = [a[8 * t : 8 * t + 8] for t in range(4)]
            r = [jnp.broadcast_to(a[k + b : k + b + 1], (8, 128)) for b in range(4)]
            p = {(i, j): take(r[i], index[j]) for i in range(4) for j in range(i, 4)}
            inv = small_inverse(p)
            rhat = [jnp.where(inside, (inner == k + b).astype(jnp.float32), r[b]) for b in range(4)]
            new_rows = [
                (inv[i][0] * rhat[0] + inv[i][1] * rhat[1]) + (inv[i][2] * rhat[2] + inv[i][3] * rhat[3])
                for i in range(4)
            ]
            fresh = []
            for t in range(4):
                c = [take(tiles[t], index[b]) for b in range(4)]
                v = jnp.where(inside, 0.0, tiles[t])
                v = v - ((c[0] * new_rows[0] + c[1] * new_rows[1]) + (c[2] * new_rows[2] + c[3] * new_rows[3]))
                if t == tile:
                    for b in range(4):
                        v = jnp.where(rows == (k + b) % 8, new_rows[b], v)
                fresh.append(v)
            out.append(jnp.concatenate(fresh, 0))
        arrays = out
    return arrays


def solve_kernel(
    count, group, place_ref, all_ref, z_ref, k_ref, st_ref, rs_ref, up_ref, down_ref, g_ref, coeff_ref, out_ref, aug, xa, xb
):
    lanes = lax.broadcasted_iota(jnp.int32, (32, 128), 1)
    rows = lax.broadcasted_iota(jnp.int32, (32, 128), 0)
    low = lanes < NV
    unit_pad = ((lanes == rows) & (rows >= NV)).astype(jnp.float32)
    unit_full = (lanes == rows).astype(jnp.float32)
    blank = jnp.zeros((32, 128), jnp.float32)

    nxt = None
    for m in reversed(range(count)):
        t = all_ref[m]
        q = jnp.where(lanes < 64, jnp.concatenate([t, pltpu.roll(t, 64, 1)], 0), 0.0)
        if nxt is None:
            aug[m] = q
        else:
            lt = jnp.transpose(nxt[:, 32:64])
            up = jnp.concatenate([jnp.zeros((32, 64), jnp.float32), lt, jnp.zeros((32, 32), jnp.float32)], 1)
            aug[m] = q + up
        nxt = q

    def invert_four(blocks):
        total = None
        for g in range(4):
            d = unit_full if blocks[g] is None else jnp.where(low, blocks[g], unit_pad)
            d = d if g == 0 else pltpu.roll(d, 32 * g, 1)
            total = d if total is None else total + d
        return total

    def spread(inverse, g, b):
        zeros = jnp.zeros_like(b)
        rhs = jnp.concatenate([zeros] * g + [b] + [zeros] * (3 - g), 0)
        return jnp.dot(inverse, rhs, precision=precise, preferred_element_type=jnp.float32)

    def arranged(a):
        ba = jnp.where(low, pltpu.roll(a, 64, 1), jnp.where(lanes < 64, a, 0.0))
        bb = jnp.where(low, pltpu.roll(a, 96, 1), jnp.where((lanes == NV) | (lanes >= 64), a, 0.0))
        return jnp.concatenate([ba, bb], 1)

    n = count
    base = 0
    offsets = []
    while n > 1:
        half = n // 2
        offsets.append(base)
        packs = (half + 3) // 4
        step = min(group, packs)

        def eliminate_group(t, _, base=base, step=step, half=half):
            sets = []
            for s in range(step):
                first = (t * step + s) * 4
                sets.append([aug[2 * (first + g)] if g < half else None for g in range(4)])
            inverses = invert_packed([invert_four(b) for b in sets])
            for s in range(step):
                first = (t * step + s) * 4
                for g in range(min(4, half)):
                    x = spread(inverses[s], g, arranged(sets[s][g]))
                    xa[base + first + g] = x[:, :128]
                    xb[base + first + g] = x[:, 128:]
            return 0

        if packs == step:
            eliminate_group(0, 0)
        else:
            lax.fori_loop(0, packs // step, eliminate_group, 0)
        keep = lanes < NV + 1
        for j in range(half):
            a = aug[2 * j + 1]
            right = xb[base + j + 1] if j + 1 < half else blank
            rhs = jnp.concatenate([blank, xa[base + j], right, blank], 0)
            aug[j] = jnp.where(keep, a, 0.0) - jnp.dot(a, rhs, precision=precise, preferred_element_type=jnp.float32)
        base += half
        n = half
    last = aug[0]
    (inverse,) = invert_packed([invert_four([last, None, None, None])])
    last = spread(inverse, 0, jnp.where(lanes == NV, last, 0.0))
    row_id = lax.broadcasted_iota(jnp.int32, (8, 128), 0)
    lane8 = lax.broadcasted_iota(jnp.int32, (8, 128), 1)
    unit = (lane8 == NV).astype(jnp.float32)

    def in_row(v, x):
        return lax.dot_general(v, x, NT, precision=precise, preferred_element_type=jnp.float32)

    pos = place_ref[0]
    zero = jnp.zeros((8, 128), jnp.float32)
    root = jnp.concatenate([in_row(unit, last), jnp.zeros((8, 96), jnp.float32)], 1)
    window = [zero, root, zero]
    for depth in reversed(range(len(offsets))):
        half = count >> (depth + 1)
        here = pos >> depth
        c = here >> 1
        if half > 1:
            start = jnp.minimum(c, half - 2)
            x2 = xa[pl.ds(offsets[depth] + start, 2)].reshape(64, 128)
            va = unit - pltpu.roll(window[0], 32, 1) - window[1]
            vb = unit - pltpu.roll(window[1], 32, 1) - window[2]
            v = jnp.where(row_id == 0, va, vb)
            y = in_row(v, x2)
            y = jnp.concatenate([y, jnp.zeros((8, 64), jnp.float32)], 1)
            lo = jnp.where(lane8 < 32, y, 0.0)
            hi = jnp.where(lane8 < 32, pltpu.roll(y, 96, 1), 0.0)
            ea = jnp.where(c == start, lo[0:1], hi[0:1])
            eb = jnp.where(c == start, hi[1:2], zero[1:2])
        else:
            va = unit - window[1]
            y = jnp.concatenate([in_row(va, xa[offsets[depth]]), jnp.zeros((8, 96), jnp.float32)], 1)
            ea, eb = y[0:1], zero[0:1]
        ea = jnp.broadcast_to(ea, (8, 128))
        eb = jnp.broadcast_to(eb, (8, 128))
        odd = (here & 1) == 1
        window = [
            jnp.where(odd, ea, window[0]),
            jnp.where(odd, window[1], ea),
            jnp.where(odd, eb, window[1]),
        ]
    coeff_ref[...] = window[1][0:1, :NV]
    finish(place_ref, window, z_ref, k_ref, st_ref, rs_ref, up_ref, down_ref, g_ref, out_ref)


def finish(place_ref, window, z_ref, k_ref, st_ref, rs_ref, up_ref, down_ref, g_ref, out_ref):
    vectors, nx, ny = z_ref.shape
    own, owners = place_ref[1], g_ref.shape[0]
    lane8 = iota((8, 128), 1)
    mine = window[1]
    weights = [take(mine, jnp.full((8, 128), v, jnp.int32)) for v in range(vectors)]
    field = None
    for v in range(vectors):
        w = weights[v]
        w = jnp.concatenate([jnp.concatenate([w] * (ny // 128), 1)] * (nx // 8), 0)
        term = w * z_ref[v]
        field = term if field is None else field + term
    k = k_ref[...]

    def in_row(row, block):
        return jnp.dot(row[:, :32], block, precision=precise, preferred_element_type=jnp.float32)

    body = iota((32, ny), 0) < NV
    f_up = in_row(window[0], jnp.where(body, up_ref[...], 0.0))[0:1]
    f_down = in_row(window[2], jnp.where(body, down_ref[...], 0.0))[0:1]
    k_up, k_down = up_ref[NV : NV + 1], down_ref[NV : NV + 1]

    def beside(o, side, there):
        block = g_ref[o, 16:48, :]
        f_row = in_row(mine, jnp.where(iota((32, 128), 0) < NV, block, 0.0))
        f_row = jnp.where(there, jnp.broadcast_to(f_row[0:1], (8, 128)), 0.0)
        k_row = jnp.where(there, jnp.broadcast_to(block[NV : NV + 1], (8, 128)), 0.0)
        f_col, k_col = [], []
        for g in range(nx // 8):
            at = lane8 == 16 * iota((8, 128), 0) + 8 * side + g
            f_col.append(jnp.sum(jnp.where(at, f_row, 0.0), 1, keepdims=True))
            k_col.append(jnp.sum(jnp.where(at, k_row, 0.0), 1, keepdims=True))
        return jnp.concatenate(f_col, 0), jnp.concatenate(k_col, 0)

    f_left, k_left = beside(jnp.maximum(own - 1, 0), 1, own > 0)
    f_right, k_right = beside(jnp.minimum(own + 1, owners - 1), 0, own < owners - 1)
    row, lane = iota((nx, ny), 0), iota((nx, ny), 1)
    east, west, north, south = row == nx - 1, row == 0, lane == ny - 1, lane == 0

    def flow(shift, axis, edge, f_edge, k_edge):
        f_near = jnp.where(edge, f_edge, pltpu.roll(field, shift, axis))
        k_near = jnp.where(edge, k_edge, pltpu.roll(k, shift, axis))
        return transmit(k, k_near) * (field - f_near)

    applied = st_ref[...] * field
    applied = applied + flow(nx - 1, 0, east, f_down, k_down)
    applied = applied + flow(1, 0, west, f_up, k_up)
    applied = applied + flow(ny - 1, 1, north, f_right, k_right)
    applied = applied + flow(1, 1, south, f_left, k_left)
    out_ref[...] = rs_ref[...] - applied


def solve(place, gathered, z, k, st, rs, up, down, g, group=8):
    count = gathered.shape[0]
    nx, ny = k.shape
    return pl.pallas_call(
        functools.partial(solve_kernel, count, group),
        out_shape=[f32(1, NV), f32(nx, ny)],
        in_specs=[SMEM] + [VMEM] * 8,
        out_specs=[VMEM, VMEM],
        scratch_shapes=[pltpu.VMEM((count, 32, 128), jnp.float32)] * 3,
        compiler_params=limit(32),
        name="solve",
    )(place, gathered, z, k, st, rs, up, down, g)


def per_device(deflation, permeability_base, design_mask, storage, right_side):
    subs, owners = lax.axis_size("sub"), lax.axis_size("own")
    k, first, last = edges(deflation, permeability_base, design_mask)
    ahead = [(i, i + 1) for i in range(subs - 1)]
    up = lax.ppermute(last, "sub", ahead)
    down = lax.ppermute(first, "sub", [(j, i) for i, j in ahead])
    p, c = assemble(deflation, k, storage, right_side)
    share = rim(first, last, up, down, p, c, owners)
    g = lax.all_to_all(share, "own", 0, 0)
    gathered = lax.all_to_all(total(g, subs), "sub", 0, 0)
    place = jnp.stack([lax.axis_index("sub"), lax.axis_index("own")]).astype(jnp.int32)
    return tuple(solve(place, gathered, deflation, k, storage, right_side, up, down, g))


def solution(mesh):
    fields = P("sub", "own")
    return jax.shard_map(
        per_device,
        mesh=mesh,
        in_specs=(P(None, "sub", "own"), fields, fields, fields, fields),
        out_specs=(P("sub", None), fields),
        check_vma=False,
    )
```

profile of v0, /device:TPU:8, one launch (start us, length us, event | category | flops | bytes accessed | tf_op | source)
XLA Modules:
  0.0 98.7 jit_solution(7970241499966456818)
XLA Ops:
  0.6 0.0 copy-start
  0.6 0.0 copy-start.6
  0.7 0.0 copy-start.7
  0.7 2.7 %edges.1 = (f32[64,256]{1,0:T(8,128)}, f32[32,256]{1,0:T(8,128)}, f32[32,256]{1,0:T(8,128)}) custom-call(f32[30,64,256]{2,1,0:T(8,128)} %z_ref.5, f32[64,256]{1,0:T(8,128)} %base_ref.1, s32[64,256]{1,0:T(8,128)} %mask_ref.1), custom_call_target="tpu_custom_call" | custom-call | tf_op jit(solution)/shard_map/edges/pallas_call | solution.py:64
  3.4 3.5 %collective-permute-start = (f32[32,256]{1,0:T(8,128)}, f32[32,256]{1,0:T(8,128)S(1)}, u32[]{:S(2)}, u32[]{:S(2)}) collective-permute-start(f32[32,256]{1,0:T(8,128)} %get-tuple-element.8.last_ref), channel_id=1, source_target_pairs={{0,8},{8,16},{16,24},{24,32},{32,40},{40,48},{48,56},{56,64},{64,7... | collective-permute-start | bytes 98312 | tf_op jit(solution)/shard_map/ppermute | solution.py:468
  6.9 5.5 %collective-permute-start.1 = (f32[32,256]{1,0:T(8,128)}, f32[32,256]{1,0:T(8,128)S(1)}, u32[]{:S(2)}, u32[]{:S(2)}) collective-permute-start(f32[32,256]{1,0:T(8,128)} %get-tuple-element.7.first_ref), channel_id=1, source_target_pairs={{8,0},{16,8},{24,16},{32,24},{40,32},{48,40},{56,48},{64,56},{72,6... | collective-permute-start | bytes 98312 | tf_op jit(solution)/shard_map/ppermute | solution.py:469
  12.4 0.0 copy-done
  12.4 0.0 copy-done.6
  12.5 0.0 copy-done.7
  12.5 0.0 copy-start.8
  12.5 0.8 copy-done.8
  13.3 6.3 %assemble.1 = (f32[32,128]{1,0:T(8,128)S(1)}, f32[32,128]{1,0:T(8,128)S(1)}) custom-call(f32[30,64,256]{2,1,0:T(8,128)S(1)} %copy-done, f32[64,256]{1,0:T(8,128)S(1)} %copy-done.8, f32[64,256]{1,0:T(8,128)S(1)} %copy-done.6, f32[64,256]{1,0:T(8,128)S(1)} %copy-done.7), custom_call_target="tpu_custom_call" | custom-call | flops 1610612736 | bytes 2097152 | tf_op jit(solution)/shard_map/assemble/pallas_call | solution.py:133
  19.6 0.0 copy-start.10
  19.6 0.6 copy-done.10
  20.2 0.0 copy-start.11
  20.2 0.6 copy-done.11
  20.8 0.0 copy-start.9
  20.8 0.0 collective-permute-done.up_ref
  20.8 0.0 copy-start.2
  20.8 0.0 collective-permute-done.1.down_ref
  20.9 0.0 copy-start.4
  20.9 0.6 copy-done.2
  21.5 0.0 copy-done.4
  21.5 1.8 %rim.1 = f32[8,48,128]{2,1,0:T(8,128)} custom-call(f32[32,256]{1,0:T(8,128)} %get-tuple-element.7.first_ref, f32[32,256]{1,0:T(8,128)} %get-tuple-element.8.last_ref, f32[32,256]{1,0:T(8,128)} %copy-done.2, f32[32,256]{1,0:T(8,128)} %copy-done.4, f32[32,128]{1,0:T(8,128)} %copy-done.10, f32[32,128]{1,0:T(8,128)} %copy-done.11), custom_call_target="tpu_custom_call" | custom-call | tf_op jit(solution)/shard_map/rim/pallas_call | solution.py:170
  23.2 0.0 copy-start.3
  23.2 0.0 copy-start.5
  23.2 11.0 %all_to_all.10.g_ref = f32[8,48,128]{2,1,0:T(8,128)} all-to-all(f32[8,48,128]{2,1,0:T(8,128)} %rim.1), channel_id=1, replica_groups=mesh['sub'=64,'own'=8] {'own'}, dimensions={0} | all-to-all | bytes 393216 | tf_op jit(solution)/shard_map/all_to_all | solution.py:472
  34.2 2.2 %total.1 = f32[64,16,128]{2,1,0:T(8,128)} custom-call(f32[8,48,128]{2,1,0:T(8,128)} %all_to_all.10.g_ref), custom_call_target="tpu_custom_call" | custom-call | tf_op jit(solution)/shard_map/total/pallas_call | solution.py:205
  36.4 15.2 %all-to-all-start.1 = ((f32[64,16,128]{2,1,0:T(8,128)}), f32[64,16,128]{2,1,0:T(8,128)S(1)}, u32[]{:S(2)}, u32[]{:S(2)}) async-start(f32[64,16,128]{2,1,0:T(8,128)} %total.1), calls=%async_computation.1 | async-start | bytes 1048576 | tf_op jit(solution)/shard_map/all_to_all | solution.py:473
  51.6 0.1 pad_add_fusion.place_ref
  51.6 18.9 %all-to-all-done.1.all_ref = f32[64,16,128]{2,1,0:T(8,128)S(1)} async-done(((f32[64,16,128]{2,1,0:T(8,128)}), f32[64,16,128]{2,1,0:T(8,128)S(1)}, u32[]{:S(2)}, u32[]{:S(2)}) %all-to-all-start.1) | async-done | bytes 524320 | tf_op jit(solution)/shard_map/all_to_all | solution.py:473
  70.6 0.0 copy-done.9
  70.6 0.0 copy-done.3
  70.6 0.0 copy-done.5
  70.6 0.0 copy-start.1
  70.6 0.9 copy-done.1
  71.5 27.1 %solve.1 = (f32[1,30]{1,0:T(1,128)}, f32[64,256]{1,0:T(8,128)}) custom-call(s32[2]{0:T(128)S(1)} %pad_add_fusion.place_ref, f32[64,16,128]{2,1,0:T(8,128)S(1)} %all-to-all-done.1.all_ref, f32[30,64,256]{2,1,0:T(8,128)S(1)} %copy-done, f32[64,256]{1,0:T(8,128)S(1)} %copy-done.9, f32[64,256]{1,0:T(8,128)S(1)} %copy-done.6, f32[64,256]{1,0:T(8,128)S(1)} %copy-done.7, ...), custom_call_target="tpu_custom_call" | custom-call | tf_op jit(solution)/shard_map/solve/pallas_call | solution.py:453
Async XLA Ops:
  0.6 11.8 %copy-start = (f32[30,64,256]{2,1,0:T(8,128)S(1)}, f32[30,64,256]{2,1,0:T(8,128)}, u32[]{:S(2)}) copy-start(f32[30,64,256]{2,1,0:T(8,128)} %z_ref.5) | copy-start | bytes 5898244
  0.6 11.8 %copy-start.6 = (f32[64,256]{1,0:T(8,128)S(1)}, f32[64,256]{1,0:T(8,128)}, u32[]{:S(2)}) copy-start(f32[64,256]{1,0:T(8,128)} %st_ref.3) | copy-start | bytes 196612
  0.7 11.8 %copy-start.7 = (f32[64,256]{1,0:T(8,128)S(1)}, f32[64,256]{1,0:T(8,128)}, u32[]{:S(2)}) copy-start(f32[64,256]{1,0:T(8,128)} %rs_ref.3) | copy-start | bytes 196612
  3.4 17.4 %collective-permute-start = (f32[32,256]{1,0:T(8,128)}, f32[32,256]{1,0:T(8,128)S(1)}, u32[]{:S(2)}, u32[]{:S(2)}) collective-permute-start(f32[32,256]{1,0:T(8,128)} %get-tuple-element.8.last_ref), channel_id=1, source_target_pairs={{0,8},{8,16},{16,24},{24,32},{32,40},{40,48},{48,56},{56,64},{64,7... | collective-permute-start | bytes 98312 | tf_op jit(solution)/shard_map/ppermute | solution.py:468
  6.9 14.0 %collective-permute-start.1 = (f32[32,256]{1,0:T(8,128)}, f32[32,256]{1,0:T(8,128)S(1)}, u32[]{:S(2)}, u32[]{:S(2)}) collective-permute-start(f32[32,256]{1,0:T(8,128)} %get-tuple-element.7.first_ref), channel_id=1, source_target_pairs={{8,0},{16,8},{24,16},{32,24},{40,32},{48,40},{56,48},{64,56},{72,6... | collective-permute-start | bytes 98312 | tf_op jit(solution)/shard_map/ppermute | solution.py:469
  12.5 0.8 copy-start.8
  19.6 0.6 copy-start.10
  20.2 0.6 copy-start.11
  20.8 49.7 %copy-start.9 = (f32[64,256]{1,0:T(8,128)S(1)}, f32[64,256]{1,0:T(8,128)}, u32[]{:S(2)}) copy-start(f32[64,256]{1,0:T(8,128)} %get-tuple-element.9.k_ref) | copy-start | bytes 196612
  20.8 0.6 copy-start.2
  20.9 0.6 copy-start.4
  23.2 47.4 %copy-start.3 = (f32[32,256]{1,0:T(8,128)S(1)}, f32[32,256]{1,0:T(8,128)}, u32[]{:S(2)}) copy-start(f32[32,256]{1,0:T(8,128)} %copy-done.2) | copy-start | bytes 98308
  23.2 47.4 %copy-start.5 = (f32[32,256]{1,0:T(8,128)S(1)}, f32[32,256]{1,0:T(8,128)}, u32[]{:S(2)}) copy-start(f32[32,256]{1,0:T(8,128)} %copy-done.4) | copy-start | bytes 98308
  36.4 34.2 %all-to-all-start.1 = ((f32[64,16,128]{2,1,0:T(8,128)}), f32[64,16,128]{2,1,0:T(8,128)S(1)}, u32[]{:S(2)}, u32[]{:S(2)}) async-start(f32[64,16,128]{2,1,0:T(8,128)} %total.1), calls=%async_computation.1 | async-start | bytes 1048576 | tf_op jit(solution)/shard_map/all_to_all | solution.py:473
  70.6 0.9 copy-start.1
where the time goes:
time: 99.2 us; the launch traced here: 98.7 us
  Pallas kernels  40.1 us (40%)
  starting transfers between devices  24.2 us (24%)
  waiting for transfers between devices  18.9 us (19%)
  blocking collectives  11 us (11%)
  local copies, waits for them, and re-layouts  3.58 us (4%)
    pallas_call x1, Pallas kernels, solve(): pl.pallas_call(functools.partial(solve_kernel, count, group), out_shape=[...  27.1 us
    all_to_all x1, waiting for transfers between devices, per_device(): gathered = lax.all_to_all(total(g, subs), 'sub', 0, 0)  18.9 us
    all_to_all x1, starting transfers between devices, per_device(): gathered = lax.all_to_all(total(g, subs), 'sub', 0, 0)  15.2 us
    all_to_all x1, blocking collectives, per_device(): g = lax.all_to_all(share, 'own', 0, 0)  11 us
    pallas_call x1, Pallas kernels, assemble(): pl.pallas_call(assemble_kernel, out_shape=[f32(32, 128), f32(32, 128)], i...  6.31 us
    ppermute x1, starting transfers between devices, per_device(): down = lax.ppermute(first, 'sub', [(j, i) for i, j in ahead])  5.54 us
    unnamed x24, local copies, waits for them, and re-layouts  3.58 us
    ppermute x1, starting transfers between devices, per_device(): up = lax.ppermute(last, 'sub', ahead)  3.48 us
  transfers between devices with their start and end apart: 3, of which 1 were waited for; matrix products, arithmetic and copies ran while one was open for 0% of the time, Pallas kernels for 6%

commit v1 on v0

--- a/solution.py
+++ b/solution.py
@@ -71,6 +71,7 @@
             pltpu.VMEM((vectors, 8, ny), jnp.float32),
             pltpu.SemaphoreType.DMA((2,)),
         ],
+        compiler_params=limit(4),
         name="edges",
     )(z, base, mask)
 
@@ -136,7 +137,7 @@
         in_specs=[VMEM] * 4,
         out_specs=[VMEM, VMEM],
         scratch_shapes=[pltpu.VMEM((vectors + 2, nx, ny), jnp.float32)],
-        compiler_params=limit(32),
+        compiler_params=limit(16),
         cost_estimate=pl.CostEstimate(flops=6 * 2 * 256 * 256 * 256 * 8, bytes_accessed=2 * 1024 * 1024, transcendentals=0),
         name="assemble",
     )(z, k, st, rs)
@@ -172,17 +173,18 @@
         out_shape=f32(copies, 48, 128),
         in_specs=[VMEM] * 6,
         out_specs=VMEM,
+        compiler_params=limit(4),
         name="rim",
     )(first, last, up, down, p, c)
 
 
-def total_kernel(g_ref, out_ref):
+def total_kernel(place_ref, g_ref, out_ref):
     count = g_ref.shape[0]
     tile = g_ref[0, :16, :]
     for o in range(1, count):
         tile = tile + g_ref[o, :16, :]
-    lane = iota((32, 128), 1)
-    used = (((lane >> 3) & 1) == 0) & (iota((32, 128), 0) < NV)
+    lane, row = iota((32, 128), 1), iota((32, 128), 0)
+    used = (((lane >> 3) & 1) == 0) & (row < NV)
     steps, flows = [], []
     for o in range(count - 1):
         here = pltpu.roll(g_ref[o, 16:48, :], 120, 1)
@@ -191,43 +193,56 @@
         step = jnp.where(used, there - here, 0.0)
         steps.append(step)
         flows.append(jnp.where(used, t * step, 0.0))
+    tile = jnp.concatenate([tile, pltpu.roll(tile, 64, 1)], 0)
     if steps:
         right = jnp.concatenate([jnp.concatenate(steps, 1), jnp.zeros((96, 128 * len(steps)), jnp.float32)], 0)
         faces = lax.dot_general(
             jnp.concatenate(flows, 1), right, NT, precision=precise, preferred_element_type=jnp.float32
         )
-        tile = tile + pack(faces)
+        tile = tile + faces
+    diag, inner = lane < NV, lane & 31
+    (inverse,) = invert_packed([jnp.where(diag, tile, 0.0) + jnp.where((lane >= NV) & (inner == row), 1.0, 0.0)])
+    right_side = jnp.sum(jnp.where(lane == NV, tile, 0.0), 1, keepdims=True)
+    right_row = jnp.sum(jnp.where(lane == row, jnp.broadcast_to(right_side, (32, 128)), 0.0), 0, keepdims=True)
+    even_diag = jnp.where(row < NV, inverse, jnp.where(row == NV, jnp.broadcast_to(right_row, (32, 128)), 0.0))
+    before = pltpu.roll(tile, 96, 1)[:, :32]
+    back = jnp.concatenate([jnp.transpose(before), jnp.zeros((32, 96), jnp.float32)], 1)
+    even = jnp.where(lane < 32, back, jnp.where(lane < 32 + NV, pltpu.roll(even_diag, 32, 1), 0.0))
+    odd = jnp.where(lane < 32, pltpu.roll(tile, 96, 1), jnp.where(lane < 64, pltpu.roll(tile, 32, 1), 0.0))
+    both = jnp.where((place_ref[0] & 1) == 0, even, odd)
+    top, bottom = both[:16], both[16:]
+    half = iota((16, 128), 1)
+    packed = jnp.where(
+        half < 32,
+        top,
+        jnp.where(half < 64, pltpu.roll(bottom, 32, 1), jnp.where(half < 96, pltpu.roll(top, 32, 1), pltpu.roll(bottom, 64, 1))),
+    )
     for s in range(out_ref.shape[0]):
-        out_ref[s] = tile
-
-
-def total(g, copies):
+        out_ref[s] = packed
+
+
+def total(place, g, copies):
     return pl.pallas_call(
         total_kernel,
         out_shape=f32(copies, 16, 128),
-        in_specs=[VMEM],
+        in_specs=[SMEM, VMEM],
         out_specs=VMEM,
+        compiler_params=limit(4),
         name="total",
-    )(g)
-
-
-def reciprocal(x):
-    r = pl.reciprocal(x, approx=True)
-    r = r * (2.0 - x * r)
-    return r * (2.0 - x * r)
+    )(place, g)
 
 
 def small_inverse(p):
     a00, a01, a11 = p[0, 0], p[0, 1], p[1, 1]
     b02, b03, b12, b13 = p[0, 2], p[0, 3], p[1, 2], p[1, 3]
-    ia = reciprocal(a00 * a11 - a01 * a01)
+    ia = 1.0 / (a00 * a11 - a01 * a01)
     h00, h01, h11 = a11 * ia, a01 * ia, a00 * ia
     w02, w03 = h00 * b02 - h01 * b12, h00 * b03 - h01 * b13
     w12, w13 = h11 * b12 - h01 * b02, h11 * b13 - h01 * b03
     s22 = p[2, 2] - (b02 * w02 + b12 * w12)
     s23 = p[2, 3] - (b02 * w03 + b12 * w13)
     s33 = p[3, 3] - (b03 * w03 + b13 * w13)
-    iz = reciprocal(s22 * s33 - s23 * s23)
+    iz = 1.0 / (s22 * s33 - s23 * s23)
     i22, i23, i33 = s33 * iz, -(s23 * iz), s22 * iz
     i02, i03 = -(w02 * i22 + w03 * i23), -(w02 * i23 + w03 * i33)
     i12, i13 = -(w12 * i22 + w13 * i23), -(w12 * i23 + w13 * i33)
@@ -274,94 +289,184 @@
     return arrays
 
 
+def three(x):
+    high = x.astype(jnp.bfloat16).astype(jnp.float32)
+    rest = x - high
+    middle = rest.astype(jnp.bfloat16).astype(jnp.float32)
+    return high, middle, rest - middle
+
+
+def narrow(*parts):
+    return jnp.concatenate([p.astype(jnp.bfloat16) for p in parts], 1)
+
+
+def six_left(x, lanes):
+    h, m, l = three(x)
+    return narrow(jnp.where(lanes < 96, h, m), jnp.where(lanes < 32, m, l)[:, :64])
+
+
+def six_right(x, lanes):
+    h, m, l = three(x)
+    one = jnp.where(lanes < 32, h, jnp.where(lanes < 64, m, jnp.where(lanes < 96, l, h)))
+    return narrow(one, jnp.where(lanes < 32, m, h)[:, :64])
+
+
+def six_rows(x):
+    h, m, l = (p.astype(jnp.bfloat16) for p in three(x))
+    return jnp.concatenate([h, m, l, h, m, h], 0)
+
+
+def six_left_64(x, lanes):
+    h, m, l = three(x)
+    return narrow(h, jnp.where(lanes < 64, h, m), jnp.where(lanes < 64, m, l))
+
+
+def six_rows_64(x):
+    h, m, l = (p.astype(jnp.bfloat16) for p in three(x))
+    return jnp.concatenate([h, m, l, h, m, h], 0)
+
+
 def solve_kernel(
-    count, group, place_ref, all_ref, z_ref, k_ref, st_ref, rs_ref, up_ref, down_ref, g_ref, coeff_ref, out_ref, aug, xa, xb
+    count,
+    place_ref,
+    all_ref,
+    z_ref,
+    k_ref,
+    st_ref,
+    rs_ref,
+    up_ref,
+    down_ref,
+    g_ref,
+    coeff_ref,
+    out_ref,
+    aug,
+    xa,
+    xb,
+    coupling,
 ):
-    lanes = lax.broadcasted_iota(jnp.int32, (32, 128), 1)
-    rows = lax.broadcasted_iota(jnp.int32, (32, 128), 0)
-    low = lanes < NV
+    lanes = iota((32, 128), 1)
+    rows = iota((32, 128), 0)
+    inner = lanes & 31
+    blank = jnp.zeros((32, 128), jnp.float32)
+    body = rows < NV
+    diag_lanes = (lanes >= 64) & (lanes < 64 + NV)
+    rhs_lane = lanes == 64 + NV
+    kept = diag_lanes | rhs_lane
+    below_32, below_64 = lanes < 32, lanes < 64
+    flat = (((1,), (0,)), ((), ()))
+
+    def dot(a, b, dims=flat):
+        return lax.dot_general(a, b, dims, preferred_element_type=jnp.float32)
+
+    def unpack(m):
+        t = all_ref[m]
+        return jnp.where((lanes & 32) == 0, jnp.concatenate([t, pltpu.roll(t, 96, 1)], 0), 0.0)
+
+    def for_all(total, body_fn, width=16):
+        if total <= width:
+            for i in range(total):
+                body_fn(i)
+        else:
+
+            def step(t, _):
+                for i in range(width):
+                    body_fn(t * width + i)
+                return 0
+
+            lax.fori_loop(0, total // width, step, 0)
+
+    half = count // 2
+    index32 = inner
+    index_d = 64 + inner
+
+    def first_spread(j):
+        even, odd = unpack(2 * j), unpack(2 * j + 1)
+        inverse = take(even, index_d)
+        back = take(even, index32)
+        ahead = take(odd, index32)
+        right_row = jnp.broadcast_to(inverse[NV : NV + 1], (32, 128))
+        left = six_left(jnp.where(body, inverse, 0.0), lanes)
+        tb, ta, tr = six_right(back, lanes), six_right(ahead, lanes), six_right(right_row, lanes)
+        is_r = iota((32, 192), 0) == NV
+        zero = jnp.zeros((32, 192), jnp.bfloat16)
+
+        def with_r(t):
+            return jnp.where(is_r, tr.astype(jnp.float32), t.astype(jnp.float32)).astype(jnp.bfloat16)
+
+        right = jnp.concatenate([tb, zero, with_r(ta), zero, zero, ta, with_r(tb), zero], 0)
+        x = dot(left, right, NT)
+        xa[j] = x[:, :128]
+        xb[j] = x[:, 128:]
+        aug[j] = odd
+        coupling[j] = jnp.where((lanes & 63) < 32, ahead, 0.0)
+        coupling[count + j] = jnp.where((lanes & 63) < 32, 0.0, back)
+
+    for_all(half, first_spread)
+    xb[half] = blank
+    coupling[count + half] = blank
+
+    def first_update(j):
+        pair = coupling[j] + coupling[count + j + 1]
+        x = jnp.concatenate([xa[j], xb[j + 1]], 0)
+        aug[j] = jnp.where(kept, aug[j], 0.0) - dot(six_left_64(pair, lanes), six_rows_64(x))
+
+    for_all(half, first_update)
+
+    offsets = [0]
+    base = half
+    n = half
     unit_pad = ((lanes == rows) & (rows >= NV)).astype(jnp.float32)
     unit_full = (lanes == rows).astype(jnp.float32)
-    blank = jnp.zeros((32, 128), jnp.float32)
-
-    nxt = None
-    for m in reversed(range(count)):
-        t = all_ref[m]
-        q = jnp.where(lanes < 64, jnp.concatenate([t, pltpu.roll(t, 64, 1)], 0), 0.0)
-        if nxt is None:
-            aug[m] = q
-        else:
-            lt = jnp.transpose(nxt[:, 32:64])
-            up = jnp.concatenate([jnp.zeros((32, 64), jnp.float32), lt, jnp.zeros((32, 32), jnp.float32)], 1)
-            aug[m] = q + up
-        nxt = q
-
-    def invert_four(blocks):
+
+    def packed(blocks):
         total = None
         for g in range(4):
-            d = unit_full if blocks[g] is None else jnp.where(low, blocks[g], unit_pad)
-            d = d if g == 0 else pltpu.roll(d, 32 * g, 1)
+            if blocks[g] is None:
+                d = unit_full if g == 0 else pltpu.roll(unit_full, 32 * g, 1)
+            else:
+                d = jnp.where(diag_lanes, blocks[g], 0.0)
+                d = d if g == 2 else pltpu.roll(d, (32 * g + 64) % 128, 1)
+                d = d + (unit_pad if g == 0 else pltpu.roll(unit_pad, 32 * g, 1))
             total = d if total is None else total + d
         return total
 
-    def spread(inverse, g, b):
-        zeros = jnp.zeros_like(b)
-        rhs = jnp.concatenate([zeros] * g + [b] + [zeros] * (3 - g), 0)
-        return jnp.dot(inverse, rhs, precision=precise, preferred_element_type=jnp.float32)
-
     def arranged(a):
-        ba = jnp.where(low, pltpu.roll(a, 64, 1), jnp.where(lanes < 64, a, 0.0))
-        bb = jnp.where(low, pltpu.roll(a, 96, 1), jnp.where((lanes == NV) | (lanes >= 64), a, 0.0))
+        r32, r64 = pltpu.roll(a, 32, 1), pltpu.roll(a, 64, 1)
+        right = jnp.where(rhs_lane, a, 0.0)
+        ba = jnp.where(below_32, a, jnp.where(diag_lanes, r32, right))
+        bb = jnp.where(below_64 & ~below_32, a, jnp.where(diag_lanes, r64, right))
         return jnp.concatenate([ba, bb], 1)
 
-    n = count
-    base = 0
-    offsets = []
     while n > 1:
         half = n // 2
         offsets.append(base)
         packs = (half + 3) // 4
-        step = min(group, packs)
-
-        def eliminate_group(t, _, base=base, step=step, half=half):
-            sets = []
-            for s in range(step):
-                first = (t * step + s) * 4
-                sets.append([aug[2 * (first + g)] if g < half else None for g in range(4)])
-            inverses = invert_packed([invert_four(b) for b in sets])
-            for s in range(step):
-                first = (t * step + s) * 4
-                for g in range(min(4, half)):
-                    x = spread(inverses[s], g, arranged(sets[s][g]))
-                    xa[base + first + g] = x[:, :128]
-                    xb[base + first + g] = x[:, 128:]
-            return 0
-
-        if packs == step:
-            eliminate_group(0, 0)
-        else:
-            lax.fori_loop(0, packs // step, eliminate_group, 0)
-        keep = lanes < NV + 1
+        sets = [[aug[2 * (4 * s + g)] if 4 * s + g < half else None for g in range(4)] for s in range(packs)]
+        inverses = invert_packed([packed(b) for b in sets])
+        for s in range(packs):
+            for g in range(min(4, half)):
+                left = six_left(take(inverses[s], 32 * g + inner), lanes)
+                x = dot(left, six_rows(arranged(sets[s][g])))
+                xa[base + 4 * s + g] = x[:, :128]
+                xb[base + 4 * s + g] = x[:, 128:]
+        xb[base + half] = blank
         for j in range(half):
             a = aug[2 * j + 1]
-            right = xb[base + j + 1] if j + 1 < half else blank
-            rhs = jnp.concatenate([blank, xa[base + j], right, blank], 0)
-            aug[j] = jnp.where(keep, a, 0.0) - jnp.dot(a, rhs, precision=precise, preferred_element_type=jnp.float32)
+            pair = jnp.where(below_64, a, pltpu.roll(a, 64, 1))
+            x = jnp.concatenate([xa[base + j], xb[base + j + 1]], 0)
+            aug[j] = jnp.where(kept, a, 0.0) - dot(six_left_64(pair, lanes), six_rows_64(x))
         base += half
         n = half
+
+    row_id = iota((8, 128), 0)
+    lane8 = iota((8, 128), 1)
+    unit = (lane8 == 64 + NV).astype(jnp.float32)
     last = aug[0]
-    (inverse,) = invert_packed([invert_four([last, None, None, None])])
-    last = spread(inverse, 0, jnp.where(lanes == NV, last, 0.0))
-    row_id = lax.broadcasted_iota(jnp.int32, (8, 128), 0)
-    lane8 = lax.broadcasted_iota(jnp.int32, (8, 128), 1)
-    unit = (lane8 == NV).astype(jnp.float32)
-
-    def in_row(v, x):
-        return lax.dot_general(v, x, NT, precision=precise, preferred_element_type=jnp.float32)
-
+    (inverse,) = invert_packed([packed([last, None, None, None])])
+    root = jnp.sum(take(last, jnp.full((32, 128), 64 + NV, jnp.int32)) * inverse, 0, keepdims=True)
+    root = jnp.where(lane8 < 32, jnp.broadcast_to(root, (8, 128)), 0.0)
     pos = place_ref[0]
     zero = jnp.zeros((8, 128), jnp.float32)
-    root = jnp.concatenate([in_row(unit, last), jnp.zeros((8, 96), jnp.float32)], 1)
     window = [zero, root, zero]
     for depth in reversed(range(len(offsets))):
         half = count >> (depth + 1)
@@ -370,18 +475,19 @@
         if half > 1:
             start = jnp.minimum(c, half - 2)
             x2 = xa[pl.ds(offsets[depth] + start, 2)].reshape(64, 128)
-            va = unit - pltpu.roll(window[0], 32, 1) - window[1]
-            vb = unit - pltpu.roll(window[1], 32, 1) - window[2]
+            va = unit - window[0] - pltpu.roll(window[1], 64, 1)
+            vb = unit - window[1] - pltpu.roll(window[2], 64, 1)
             v = jnp.where(row_id == 0, va, vb)
-            y = in_row(v, x2)
+            y = lax.dot_general(v, x2, NT, precision=precise, preferred_element_type=jnp.float32)
             y = jnp.concatenate([y, jnp.zeros((8, 64), jnp.float32)], 1)
             lo = jnp.where(lane8 < 32, y, 0.0)
             hi = jnp.where(lane8 < 32, pltpu.roll(y, 96, 1), 0.0)
             ea = jnp.where(c == start, lo[0:1], hi[0:1])
             eb = jnp.where(c == start, hi[1:2], zero[1:2])
         else:
-            va = unit - window[1]
-            y = jnp.concatenate([in_row(va, xa[offsets[depth]]), jnp.zeros((8, 96), jnp.float32)], 1)
+            va = unit - pltpu.roll(window[1], 64, 1)
+            y = lax.dot_general(va, xa[offsets[depth]], NT, precision=precise, preferred_element_type=jnp.float32)
+            y = jnp.concatenate([y, jnp.zeros((8, 96), jnp.float32)], 1)
             ea, eb = y[0:1], zero[0:1]
         ea = jnp.broadcast_to(ea, (8, 128))
         eb = jnp.broadcast_to(eb, (8, 128))
@@ -447,22 +553,23 @@
     out_ref[...] = rs_ref[...] - applied
 
 
-def solve(place, gathered, z, k, st, rs, up, down, g, group=8):
+def solve(place, gathered, z, k, st, rs, up, down, g):
     count = gathered.shape[0]
     nx, ny = k.shape
     return pl.pallas_call(
-        functools.partial(solve_kernel, count, group),
+        functools.partial(solve_kernel, count),
         out_shape=[f32(1, NV), f32(nx, ny)],
         in_specs=[SMEM] + [VMEM] * 8,
         out_specs=[VMEM, VMEM],
-        scratch_shapes=[pltpu.VMEM((count, 32, 128), jnp.float32)] * 3,
-        compiler_params=limit(32),
+        scratch_shapes=[pltpu.VMEM((n, 32, 128), jnp.float32) for n in (count // 2, count, count + 1, 2 * count)],
+        compiler_params=limit(16),
         name="solve",
     )(place, gathered, z, k, st, rs, up, down, g)
 
 
 def per_device(deflation, permeability_base, design_mask, storage, right_side):
     subs, owners = lax.axis_size("sub"), lax.axis_size("own")
+    place = jnp.stack([lax.axis_index("sub"), lax.axis_index("own")]).astype(jnp.int32)
     k, first, last = edges(deflation, permeability_base, design_mask)
     ahead = [(i, i + 1) for i in range(subs - 1)]
     up = lax.ppermute(last, "sub", ahead)
@@ -470,8 +577,7 @@
     p, c = assemble(deflation, k, storage, right_side)
     share = rim(first, last, up, down, p, c, owners)
     g = lax.all_to_all(share, "own", 0, 0)
-    gathered = lax.all_to_all(total(g, subs), "sub", 0, 0)
-    place = jnp.stack([lax.axis_index("sub"), lax.axis_index("own")]).astype(jnp.int32)
+    gathered = lax.all_to_all(total(place, g, subs), "sub", 0, 0)
     return tuple(solve(place, gathered, deflation, k, storage, right_side, up, down, g))
 
 

time: 99.2 us -> 84.7 us (0.85)
  blocking collectives: 11 us -> 32.8 us
  Pallas kernels: 40.1 us -> 27.6 us
  waiting for transfers between devices: 18.9 us -> 6.68 us
  starting transfers between devices: 24.2 us -> 13.2 us
    all_to_all x1, blocking collectives: 11 us -> 32.8 us  [per_device(): gathered = lax.all_to_all(total(place, g, subs), 'sub', 0, 0)]
    all_to_all x1, waiting for transfers between devices: 18.9 us -> 6.67 us  [per_device(): g = lax.all_to_all(share, 'own', 0, 0)]
    all_to_all x1, starting transfers between devices: 15.2 us -> 3.39 us  [per_device(): g = lax.all_to_all(share, 'own', 0, 0)]
    pallas_call x2, Pallas kernels: 29.3 us -> 20.2 us  [the longest x1 17.9 us: solve(): pl.pallas_call(functools.partial(solve_kernel, count), out_shape=[f32(1,...]
    pallas_call x1, Pallas kernels: 2.73 us -> 0.14 us  [edges(): pl.pallas_call(edges_kernel, out_shape=[f32(nx, ny), f32(32, ny), f32(32,...]
    ppermute x1, starting transfers between devices: 5.54 us -> 7.86 us  [per_device(): down = lax.ppermute(first, 'sub', [(j, i) for i, j in ahead])]
    ppermute x1, starting transfers between devices: 3.48 us -> 1.92 us  [per_device(): up = lax.ppermute(last, 'sub', ahead)]
    unnamed x24 -> x12, local copies, waits for them, and re-layouts: 3.58 us -> 3.23 us
  transfers between devices with their start and end apart: 3 -> 3, of which waited for: 1 -> 1; matrix products, arithmetic and copies ran while one was open for 0% -> 0% of each run, Pallas kernels for 6% -> 7%
where the time goes in v1:
time: 84.7 us; the launch traced here: 84.3 us
  blocking collectives  32.8 us (39%)
  Pallas kernels  27.6 us (33%)
  starting transfers between devices  13.2 us (16%)
  waiting for transfers between devices  6.68 us (8%)
  local copies, waits for them, and re-layouts  3.23 us (4%)
    all_to_all x1, blocking collectives, per_device(): gathered = lax.all_to_all(total(place, g, subs), 'sub', 0, 0)  32.8 us
    pallas_call x1, Pallas kernels, solve(): pl.pallas_call(functools.partial(solve_kernel, count), out_shape=[f32(1,...  17.9 us
    ppermute x1, starting transfers between devices, per_device(): down = lax.ppermute(first, 'sub', [(j, i) for i, j in ahead])  7.86 us
    all_to_all x1, waiting for transfers between devices, per_device(): g = lax.all_to_all(share, 'own', 0, 0)  6.67 us
    pallas_call x1, Pallas kernels, assemble(): pl.pallas_call(assemble_kernel, out_shape=[f32(32, 128), f32(32, 128)], i...  6.31 us
    all_to_all x1, starting transfers between devices, per_device(): g = lax.all_to_all(share, 'own', 0, 0)  3.39 us
    unnamed x12, local copies, waits for them, and re-layouts  3.23 us
    pallas_call x1, Pallas kernels, total(): pl.pallas_call(total_kernel, out_shape=f32(copies, 16, 128), in_specs=[SM...  2.31 us
  transfers between devices with their start and end apart: 3, of which 1 were waited for; matrix products, arithmetic and copies ran while one was open for 0% of the time, Pallas kernels for 7%

profile of v1, /device:TPU:8, one launch (start us, length us, event | category | flops | bytes accessed | tf_op | source)
XLA Modules:
  0.0 84.3 jit_solution(16760786268090341494)
XLA Ops:
  0.6 0.0 copy-start
  0.6 1.5 %copy-done = f32[30,64,256]{2,1,0:T(8,128)S(1)} copy-done((f32[30,64,256]{2,1,0:T(8,128)S(1)}, f32[30,64,256]{2,1,0:T(8,128)}, u32[]{:S(2)}) %copy-start) | copy-done | bytes 1966104
  2.2 0.0 copy-start.2
  2.2 0.8 copy-done.2
  3.0 0.0 copy-start.3
  3.0 0.8 copy-done.3
  3.9 0.0 copy-start.1
  3.9 0.0 copy-start.4
  3.9 0.0 copy-start.5
  3.9 0.1 edges.1
  4.0 7.9 %collective-permute-start.1 = (f32[32,256]{1,0:T(8,128)S(1)}, f32[32,256]{1,0:T(8,128)S(1)}, u32[]{:S(2)}, u32[]{:S(2)}) collective-permute-start(f32[32,256]{1,0:T(8,128)S(1)} %get-tuple-element.7.first_ref), channel_id=1, source_target_pairs={{8,0},{16,8},{24,16},{32,24},{40,32},{48,40},{56,48},{64,56},{72,6... | collective-permute-start | bytes 98312 | tf_op jit(solution)/shard_map/ppermute | solution.py:576
  11.9 1.9 %collective-permute-start = (f32[32,256]{1,0:T(8,128)S(1)}, f32[32,256]{1,0:T(8,128)S(1)}, u32[]{:S(2)}, u32[]{:S(2)}) collective-permute-start(f32[32,256]{1,0:T(8,128)S(1)} %get-tuple-element.8.last_ref), channel_id=1, source_target_pairs={{0,8},{8,16},{16,24},{24,32},{32,40},{40,48},{48,56},{56,64},{64,7... | collective-permute-start | bytes 98312 | tf_op jit(solution)/shard_map/ppermute | solution.py:575
  13.8 0.0 copy-done.1
  13.8 0.0 copy-done.4
  13.8 0.0 copy-done.5
  13.8 6.3 %assemble.1 = (f32[32,128]{1,0:T(8,128)S(1)}, f32[32,128]{1,0:T(8,128)S(1)}) custom-call(f32[30,64,256]{2,1,0:T(8,128)S(1)} %copy-done.1, f32[64,256]{1,0:T(8,128)S(1)} %get-tuple-element.9.k_ref, f32[64,256]{1,0:T(8,128)S(1)} %copy-done.4, f32[64,256]{1,0:T(8,128)S(1)} %copy-done.5), custom_call_target="tpu_custom_call" | custom-call | flops 1610612736 | bytes 2097152 | tf_op jit(solution)/shard_map/assemble/pallas_call | solution.py:134
  20.2 0.0 collective-permute-done.1.down_ref
  20.2 0.0 collective-permute-done.up_ref
  20.2 1.0 %rim.1 = f32[8,48,128]{2,1,0:T(8,128)} custom-call(f32[32,256]{1,0:T(8,128)S(1)} %get-tuple-element.7.first_ref, f32[32,256]{1,0:T(8,128)S(1)} %get-tuple-element.8.last_ref, f32[32,256]{1,0:T(8,128)S(1)} %collective-permute-done.up_ref, f32[32,256]{1,0:T(8,128)S(1)} %collective-permute-done.1.down_ref, f32[32,128]{1,0:T(8,128)S(1)} %get-tuple-element.10.p_ref, ...), custom_call_target="tpu_custom_call" | custom-call | tf_op jit(solution)/shard_map/rim/pallas_call | solution.py:171
  21.1 3.4 %all-to-all-start = ((f32[8,48,128]{2,1,0:T(8,128)}), f32[8,48,128]{2,1,0:T(8,128)S(1)}, u32[]{:S(2)}, u32[]{:S(2)}) async-start(f32[8,48,128]{2,1,0:T(8,128)} %rim.1), calls=%async_computation | async-start | bytes 393216 | tf_op jit(solution)/shard_map/all_to_all | solution.py:579
  24.6 0.1 pad_add_fusion.place_ref
  24.6 6.7 %all-to-all-done.g_ref = f32[8,48,128]{2,1,0:T(8,128)S(1)} async-done(((f32[8,48,128]{2,1,0:T(8,128)}), f32[8,48,128]{2,1,0:T(8,128)S(1)}, u32[]{:S(2)}, u32[]{:S(2)}) %all-to-all-start) | async-done | bytes 196640 | tf_op jit(solution)/shard_map/all_to_all | solution.py:579
  31.3 2.3 %total.1 = f32[64,16,128]{2,1,0:T(8,128)S(1)} custom-call(s32[2]{0:T(128)S(1)} %pad_add_fusion.place_ref, f32[8,48,128]{2,1,0:T(8,128)S(1)} %all-to-all-done.g_ref), custom_call_target="tpu_custom_call" | custom-call | tf_op jit(solution)/shard_map/total/pallas_call | solution.py:225
  33.6 32.8 %all_to_all.10.all_ref = f32[64,16,128]{2,1,0:T(8,128)S(1)} all-to-all(f32[64,16,128]{2,1,0:T(8,128)S(1)} %total.1), channel_id=1, replica_groups=mesh['sub'=64,'own'=8] {'sub'}, dimensions={0} | all-to-all | bytes 1048576 | tf_op jit(solution)/shard_map/all_to_all | solution.py:580
  66.4 17.9 %solve.1 = (f32[1,30]{1,0:T(1,128)}, f32[64,256]{1,0:T(8,128)}) custom-call(s32[2]{0:T(128)S(1)} %pad_add_fusion.place_ref, f32[64,16,128]{2,1,0:T(8,128)S(1)} %all_to_all.10.all_ref, f32[30,64,256]{2,1,0:T(8,128)S(1)} %copy-done.1, f32[64,256]{1,0:T(8,128)S(1)} %get-tuple-element.9.k_ref, f32[64,256]{1,0:T(8,128)S(1)} %copy-done.4, ...), custom_call_target="tpu_custom_call" | custom-call | tf_op jit(solution)/shard_map/solve/pallas_call | solution.py:559
Async XLA Ops:
  0.6 1.5 %copy-start = (f32[30,64,256]{2,1,0:T(8,128)S(1)}, f32[30,64,256]{2,1,0:T(8,128)}, u32[]{:S(2)}) copy-start(f32[30,64,256]{2,1,0:T(8,128)} %z_ref.5) | copy-start | bytes 5898244
  2.2 0.8 copy-start.2
  3.0 0.8 copy-start.3
  3.9 10.0 %copy-start.1 = (f32[30,64,256]{2,1,0:T(8,128)S(1)}, f32[30,64,256]{2,1,0:T(8,128)}, u32[]{:S(2)}) copy-start(f32[30,64,256]{2,1,0:T(8,128)} %z_ref.5) | copy-start | bytes 5898244
  3.9 10.0 %copy-start.4 = (f32[64,256]{1,0:T(8,128)S(1)}, f32[64,256]{1,0:T(8,128)}, u32[]{:S(2)}) copy-start(f32[64,256]{1,0:T(8,128)} %st_ref.3) | copy-start | bytes 196612
  3.9 10.0 %copy-start.5 = (f32[64,256]{1,0:T(8,128)S(1)}, f32[64,256]{1,0:T(8,128)}, u32[]{:S(2)}) copy-start(f32[64,256]{1,0:T(8,128)} %rs_ref.3) | copy-start | bytes 196612
  4.0 16.1 %collective-permute-start.1 = (f32[32,256]{1,0:T(8,128)S(1)}, f32[32,256]{1,0:T(8,128)S(1)}, u32[]{:S(2)}, u32[]{:S(2)}) collective-permute-start(f32[32,256]{1,0:T(8,128)S(1)} %get-tuple-element.7.first_ref), channel_id=1, source_target_pairs={{8,0},{16,8},{24,16},{32,24},{40,32},{48,40},{56,48},{64,56},{72,6... | collective-permute-start | bytes 98312 | tf_op jit(solution)/shard_map/ppermute | solution.py:576
  11.9 8.3 %collective-permute-start = (f32[32,256]{1,0:T(8,128)S(1)}, f32[32,256]{1,0:T(8,128)S(1)}, u32[]{:S(2)}, u32[]{:S(2)}) collective-permute-start(f32[32,256]{1,0:T(8,128)S(1)} %get-tuple-element.8.last_ref), channel_id=1, source_target_pairs={{0,8},{8,16},{16,24},{24,32},{32,40},{40,48},{48,56},{56,64},{64,7... | collective-permute-start | bytes 98312 | tf_op jit(solution)/shard_map/ppermute | solution.py:575
  21.1 10.2 %all-to-all-start = ((f32[8,48,128]{2,1,0:T(8,128)}), f32[8,48,128]{2,1,0:T(8,128)S(1)}, u32[]{:S(2)}, u32[]{:S(2)}) async-start(f32[8,48,128]{2,1,0:T(8,128)} %rim.1), calls=%async_computation | async-start | bytes 393216 | tf_op jit(solution)/shard_map/all_to_all | solution.py:579

commit v2 on v1

--- a/solution.py
+++ b/solution.py
@@ -28,6 +28,10 @@
     return lax.broadcasted_iota(jnp.int32, shape, dim)
 
 
+def permeability(base, mask):
+    return base * jnp.exp((mask.astype(jnp.float32) - 1.0) * LOG_CONTRAST)
+
+
 def transmit(centre, beside):
     return 2.0 * centre * beside / (centre + beside)
 
@@ -40,40 +44,24 @@
     return high, middle, low
 
 
-def edges_kernel(z_ref, base_ref, mask_ref, k_ref, first_ref, last_ref, head, tail, sems):
-    nx = z_ref.shape[1]
-    vectors = z_ref.shape[0]
-    copies = [
-        pltpu.make_async_copy(z_ref.at[:, pl.ds(0, 8), :], head, sems.at[0]),
-        pltpu.make_async_copy(z_ref.at[:, pl.ds(nx - 8, 8), :], tail, sems.at[1]),
-    ]
-    for c in copies:
-        c.start()
-    k = base_ref[...] * jnp.exp((mask_ref[...].astype(jnp.float32) - 1.0) * LOG_CONTRAST)
-    k_ref[...] = k
-    for c in copies:
-        c.wait()
+def edges_kernel(z_ref, k_ref, first_ref, last_ref):
+    vectors, nx, ny = z_ref.shape
+    pad = jnp.zeros((31 - vectors, ny), jnp.float32)
+    for row, out in ((0, first_ref), (nx - 1, last_ref)):
+        rows = [z_ref[v, row : row + 1, :] for v in range(vectors)]
+        out[...] = jnp.concatenate(rows + [k_ref[row : row + 1, :], pad], 0)
+
+
+def edges(z, k):
     ny = k.shape[1]
-    pad = jnp.zeros((31 - vectors, ny), jnp.float32)
-    first_ref[...] = jnp.concatenate([head[v, 0:1, :] for v in range(vectors)] + [k[0:1]] + [pad], 0)
-    last_ref[...] = jnp.concatenate([tail[v, 7:8, :] for v in range(vectors)] + [k[nx - 1 : nx]] + [pad], 0)
-
-
-def edges(z, base, mask):
-    vectors, nx, ny = z.shape
     return pl.pallas_call(
         edges_kernel,
-        out_shape=[f32(nx, ny), f32(32, ny), f32(32, ny)],
-        in_specs=[pl.BlockSpec(memory_space=pl.ANY), VMEM, VMEM],
-        out_specs=[VMEM, VMEM, VMEM],
-        scratch_shapes=[
-            pltpu.VMEM((vectors, 8, ny), jnp.float32),
-            pltpu.VMEM((vectors, 8, ny), jnp.float32),
-            pltpu.SemaphoreType.DMA((2,)),
-        ],
+        out_shape=[f32(32, ny), f32(32, ny)],
+        in_specs=[VMEM, VMEM],
+        out_specs=[VMEM, VMEM],
         compiler_params=limit(4),
         name="edges",
-    )(z, base, mask)
+    )(z, k)
 
 
 def assemble_kernel(z_ref, k_ref, st_ref, rs_ref, p_ref, c_ref, az_ref):
@@ -91,7 +79,7 @@
         az_ref[v] = st * z - fn + pltpu.roll(fn, 1, 1) - fe + pltpu.roll(fe, 1, 0)
         return 0
 
-    lax.fori_loop(0, vectors, apply, 0, unroll=2)
+    lax.fori_loop(0, vectors, apply, 0, unroll=6)
     az_ref[vectors] = rs_ref[...]
     az_ref[vectors + 1] = jnp.zeros((nx, ny), jnp.float32)
 
@@ -256,9 +244,69 @@
     return jnp.take_along_axis(x, index, axis=1)
 
 
+def spread_row(x, row):
+    return jnp.broadcast_to(x[row : row + 1], (8, 128))
+
+
 def invert_packed(arrays):
-    lanes = lax.broadcasted_iota(jnp.int32, (8, 128), 1)
-    rows = lax.broadcasted_iota(jnp.int32, (8, 128), 0)
+    lanes = iota((8, 128), 1)
+    rows = iota((8, 128), 0)
+    start, inner = lanes & ~31, lanes & 31
+    states = []
+    for a in arrays:
+        tiles = [a[8 * t : 8 * t + 8] for t in range(4)]
+        c = [take(tiles[0], start + b) for b in range(4)]
+        states.append((tiles, {(i, j): spread_row(c[j], i) for i in range(4) for j in range(i, 4)}))
+    for k in range(0, 32, 4):
+        index = [start + (k + b) for b in range(4)]
+        inside = (inner >= k) & (inner < k + 4)
+        tile, q = k // 8, k % 8
+        out = []
+        for tiles, p in states:
+            inv = small_inverse(p)
+            cols = [[take(tiles[t], index[b]) for b in range(4)] for t in range(4)]
+            pivot = None
+            if k < 28:
+                t2, q2 = (k + 4) // 8, (k + 4) % 8
+                own = [take(tiles[t2], start + (k + 4 + b)) for b in range(4)]
+                cross = [[spread_row(cols[t2][b], q2 + i) for b in range(4)] for i in range(4)]
+                scaled = [
+                    [
+                        (inv[b][0] * cross[i][0] + inv[b][1] * cross[i][1])
+                        + (inv[b][2] * cross[i][2] + inv[b][3] * cross[i][3])
+                        for b in range(4)
+                    ]
+                    for i in range(4)
+                ]
+                pivot = {}
+                for i in range(4):
+                    for j in range(i, 4):
+                        change = (cross[i][0] * scaled[j][0] + cross[i][1] * scaled[j][1]) + (
+                            cross[i][2] * scaled[j][2] + cross[i][3] * scaled[j][3]
+                        )
+                        pivot[i, j] = spread_row(own[j], q2 + i) - change
+            rhat = [jnp.where(inside, (inner == k + b).astype(jnp.float32), spread_row(tiles[tile], q + b)) for b in range(4)]
+            new_rows = [
+                (inv[i][0] * rhat[0] + inv[i][1] * rhat[1]) + (inv[i][2] * rhat[2] + inv[i][3] * rhat[3])
+                for i in range(4)
+            ]
+            fresh = []
+            for t in range(4):
+                c = cols[t]
+                v = jnp.where(inside, 0.0, tiles[t])
+                v = v - ((c[0] * new_rows[0] + c[1] * new_rows[1]) + (c[2] * new_rows[2] + c[3] * new_rows[3]))
+                if t == tile:
+                    for b in range(4):
+                        v = jnp.where(rows == q + b, new_rows[b], v)
+                fresh.append(v)
+            out.append((fresh, pivot))
+        states = out
+    return [jnp.concatenate(tiles, 0) for tiles, _ in states]
+
+
+def invert_many(arrays):
+    lanes = iota((8, 128), 1)
+    rows = iota((8, 128), 0)
     start, inner = lanes & ~31, lanes & 31
     for k in range(0, 32, 4):
         index = [start + (k + b) for b in range(4)]
@@ -268,7 +316,11 @@
         for a in arrays:
             tiles = [a[8 * t : 8 * t + 8] for t in range(4)]
             r = [jnp.broadcast_to(a[k + b : k + b + 1], (8, 128)) for b in range(4)]
-            p = {(i, j): take(r[i], index[j]) for i in range(4) for j in range(i, 4)}
+            cols = [[take(tiles[t], index[b]) for b in range(4)] for t in range(4)]
+            q = k % 8
+            p = {
+                (i, j): spread_row(cols[tile][j], q + i) for i in range(4) for j in range(i, 4)
+            }
             inv = small_inverse(p)
             rhat = [jnp.where(inside, (inner == k + b).astype(jnp.float32), r[b]) for b in range(4)]
             new_rows = [
@@ -277,7 +329,7 @@
             ]
             fresh = []
             for t in range(4):
-                c = [take(tiles[t], index[b]) for b in range(4)]
+                c = cols[t]
                 v = jnp.where(inside, 0.0, tiles[t])
                 v = v - ((c[0] * new_rows[0] + c[1] * new_rows[1]) + (c[2] * new_rows[2] + c[3] * new_rows[3]))
                 if t == tile:
@@ -442,7 +494,7 @@
         offsets.append(base)
         packs = (half + 3) // 4
         sets = [[aug[2 * (4 * s + g)] if 4 * s + g < half else None for g in range(4)] for s in range(packs)]
-        inverses = invert_packed([packed(b) for b in sets])
+        inverses = (invert_packed if packs < 4 else invert_many)([packed(b) for b in sets])
         for s in range(packs):
             for g in range(min(4, half)):
                 left = six_left(take(inverses[s], 32 * g + inner), lanes)
@@ -570,7 +622,8 @@
 def per_device(deflation, permeability_base, design_mask, storage, right_side):
     subs, owners = lax.axis_size("sub"), lax.axis_size("own")
     place = jnp.stack([lax.axis_index("sub"), lax.axis_index("own")]).astype(jnp.int32)
-    k, first, last = edges(deflation, permeability_base, design_mask)
+    k = permeability(permeability_base, design_mask)
+    first, last = edges(deflation, k)
     ahead = [(i, i + 1) for i in range(subs - 1)]
     up = lax.ppermute(last, "sub", ahead)
     down = lax.ppermute(first, "sub", [(j, i) for i, j in ahead])

time: 84.7 us -> 80.2 us (0.947)
  Pallas kernels: 27.6 us -> 23.9 us
  local copies, waits for them, and re-layouts: 3.23 us -> 1.55 us
  other arithmetic: 0.08 us -> 1 us
    pallas_call x1, Pallas kernels: 17.9 us -> 15.2 us  [solve(): pl.pallas_call(functools.partial(solve_kernel, count), out_shape=[f32(1,...]
    unnamed x12 -> x8, local copies, waits for them, and re-layouts: 3.23 us -> 1.55 us
    mul x0 -> x1, other arithmetic: none -> 0.93 us  [permeability(): return base * jnp.exp((mask.astype(jnp.float32) - 1.0) * LOG_CONTRAST)]
where the time goes in v2:
time: 80.2 us; the launch traced here: 79.8 us
  blocking collectives  32.8 us (41%)
  Pallas kernels  23.9 us (30%)
  starting transfers between devices  13.2 us (16%)
  waiting for transfers between devices  6.68 us (8%)
  local copies, waits for them, and re-layouts  1.55 us (2%)
  other arithmetic  1 us (1%)
    all_to_all x1, blocking collectives, per_device(): gathered = lax.all_to_all(total(place, g, subs), 'sub', 0, 0)  32.8 us
    pallas_call x1, Pallas kernels, solve(): pl.pallas_call(functools.partial(solve_kernel, count), out_shape=[f32(1,...  15.2 us
    ppermute x1, starting transfers between devices, per_device(): down = lax.ppermute(first, 'sub', [(j, i) for i, j in ahead])  7.86 us
    all_to_all x1, waiting for transfers between devices, per_device(): g = lax.all_to_all(share, 'own', 0, 0)  6.67 us
    pallas_call x1, Pallas kernels, assemble(): pl.pallas_call(assemble_kernel, out_shape=[f32(32, 128), f32(32, 128)], i...  5.88 us
    all_to_all x1, starting transfers between devices, per_device(): g = lax.all_to_all(share, 'own', 0, 0)  3.39 us
    ppermute x1, starting transfers between devices, per_device(): up = lax.ppermute(last, 'sub', ahead)  1.92 us
    pallas_call x1, Pallas kernels, total(): pl.pallas_call(total_kernel, out_shape=f32(copies, 16, 128), in_specs=[SM...  1.86 us
  transfers between devices with their start and end apart: 3, of which 1 were waited for; matrix products, arithmetic and copies ran while one was open for 0% of the time, Pallas kernels for 7%

profile of v2, /device:TPU:8, one launch (start us, length us, event | category | flops | bytes accessed | tf_op | source)
XLA Modules:
  0.0 79.8 jit_solution(17303130059241349285)
XLA Ops:
  0.6 0.0 copy-start.3
  0.6 0.0 copy-start.2
  0.7 0.9 %exponential_multiply_fusion.k_ref = f32[64,256]{1,0:T(8,128)S(1)} fusion(f32[64,256]{1,0:T(8,128)} %param.6, s32[64,256]{1,0:T(8,128)} %param.7), kind=kLoop, calls=%fused_computation | loop fusion | flops 65536 | bytes 196608 | tf_op jit(solution)/shard_map/mul | solution.py:32
  1.6 0.0 copy-start
  1.6 1.5 %copy-done = f32[30,64,256]{2,1,0:T(8,128)S(1)} copy-done((f32[30,64,256]{2,1,0:T(8,128)S(1)}, f32[30,64,256]{2,1,0:T(8,128)}, u32[]{:S(2)}) %copy-start) | copy-done | bytes 1966104
  3.1 0.0 copy-start.1
  3.2 7.9 %collective-permute-start.1 = (f32[32,256]{1,0:T(8,128)S(1)}, f32[32,256]{1,0:T(8,128)S(1)}, u32[]{:S(2)}, u32[]{:S(2)}) collective-permute-start(f32[32,256]{1,0:T(8,128)S(1)} %get-tuple-element.6.first_ref), channel_id=1, source_target_pairs={{8,0},{16,8},{24,16},{32,24},{40,32},{48,40},{56,48},{64,56},{72,6... | collective-permute-start | bytes 98312 | tf_op jit(solution)/shard_map/ppermute | solution.py:629
  11.0 1.9 %collective-permute-start = (f32[32,256]{1,0:T(8,128)S(1)}, f32[32,256]{1,0:T(8,128)S(1)}, u32[]{:S(2)}, u32[]{:S(2)}) collective-permute-start(f32[32,256]{1,0:T(8,128)S(1)} %get-tuple-element.7.last_ref), channel_id=1, source_target_pairs={{0,8},{8,16},{16,24},{24,32},{32,40},{40,48},{48,56},{56,64},{64,7... | collective-permute-start | bytes 98312 | tf_op jit(solution)/shard_map/ppermute | solution.py:628
  13.0 0.0 copy-done.3
  13.0 0.0 copy-done.2
  13.0 0.0 copy-done.1
  13.0 5.9 %assemble.1 = (f32[32,128]{1,0:T(8,128)S(1)}, f32[32,128]{1,0:T(8,128)S(1)}) custom-call(f32[30,64,256]{2,1,0:T(8,128)S(1)} %copy-done.1, f32[64,256]{1,0:T(8,128)S(1)} %exponential_multiply_fusion.k_ref, f32[64,256]{1,0:T(8,128)S(1)} %copy-done.2, f32[64,256]{1,0:T(8,128)S(1)} %copy-done.3), custom_call_target="tpu_custom_call" | custom-call | flops 1610612736 | bytes 2097152 | tf_op jit(solution)/shard_map/assemble/pallas_call | solution.py:122
  18.9 0.0 collective-permute-done.1.down_ref
  18.9 0.0 collective-permute-done.up_ref
  18.9 1.0 %rim.1 = f32[8,48,128]{2,1,0:T(8,128)} custom-call(f32[32,256]{1,0:T(8,128)S(1)} %get-tuple-element.6.first_ref, f32[32,256]{1,0:T(8,128)S(1)} %get-tuple-element.7.last_ref, f32[32,256]{1,0:T(8,128)S(1)} %collective-permute-done.up_ref, f32[32,256]{1,0:T(8,128)S(1)} %collective-permute-done.1.down_ref, f32[32,128]{1,0:T(8,128)S(1)} %get-tuple-element.8.p_ref, ...), custom_call_target="tpu_custom_call" | custom-call | tf_op jit(solution)/shard_map/rim/pallas_call | solution.py:159
  19.9 3.4 %all-to-all-start = ((f32[8,48,128]{2,1,0:T(8,128)}), f32[8,48,128]{2,1,0:T(8,128)S(1)}, u32[]{:S(2)}, u32[]{:S(2)}) async-start(f32[8,48,128]{2,1,0:T(8,128)} %rim.1), calls=%async_computation | async-start | bytes 393216 | tf_op jit(solution)/shard_map/all_to_all | solution.py:632
  23.3 0.1 pad_add_fusion.place_ref
  23.3 6.7 %all-to-all-done.g_ref = f32[8,48,128]{2,1,0:T(8,128)S(1)} async-done(((f32[8,48,128]{2,1,0:T(8,128)}), f32[8,48,128]{2,1,0:T(8,128)S(1)}, u32[]{:S(2)}, u32[]{:S(2)}) %all-to-all-start) | async-done | bytes 196640 | tf_op jit(solution)/shard_map/all_to_all | solution.py:632
  30.0 1.9 %total.1 = f32[64,16,128]{2,1,0:T(8,128)S(1)} custom-call(s32[2]{0:T(128)S(1)} %pad_add_fusion.place_ref, f32[8,48,128]{2,1,0:T(8,128)S(1)} %all-to-all-done.g_ref), custom_call_target="tpu_custom_call" | custom-call | tf_op jit(solution)/shard_map/total/pallas_call | solution.py:213
  31.9 32.8 %all_to_all.10.all_ref = f32[64,16,128]{2,1,0:T(8,128)S(1)} all-to-all(f32[64,16,128]{2,1,0:T(8,128)S(1)} %total.1), channel_id=1, replica_groups=mesh['sub'=64,'own'=8] {'sub'}, dimensions={0} | all-to-all | bytes 1048576 | tf_op jit(solution)/shard_map/all_to_all | solution.py:633
  64.6 15.2 %solve.1 = (f32[1,30]{1,0:T(1,128)}, f32[64,256]{1,0:T(8,128)}) custom-call(s32[2]{0:T(128)S(1)} %pad_add_fusion.place_ref, f32[64,16,128]{2,1,0:T(8,128)S(1)} %all_to_all.10.all_ref, f32[30,64,256]{2,1,0:T(8,128)S(1)} %copy-done.1, f32[64,256]{1,0:T(8,128)S(1)} %exponential_multiply_fusion.k_ref, f32[64,256]{1,0:T(8,128)S(1)} %copy-done.2, ...), custom_call_target="tpu_custom_call" | custom-call | tf_op jit(solution)/shard_map/solve/pallas_call | solution.py:611
  (1 shorter events, 0.0 us)
Async XLA Ops:
  0.6 12.3 %copy-start.3 = (f32[64,256]{1,0:T(8,128)S(1)}, f32[64,256]{1,0:T(8,128)}, u32[]{:S(2)}) copy-start(f32[64,256]{1,0:T(8,128)} %rs_ref.3) | copy-start | bytes 196612
  0.6 12.3 %copy-start.2 = (f32[64,256]{1,0:T(8,128)S(1)}, f32[64,256]{1,0:T(8,128)}, u32[]{:S(2)}) copy-start(f32[64,256]{1,0:T(8,128)} %st_ref.3) | copy-start | bytes 196612
  1.6 1.5 %copy-start = (f32[30,64,256]{2,1,0:T(8,128)S(1)}, f32[30,64,256]{2,1,0:T(8,128)}, u32[]{:S(2)}) copy-start(f32[30,64,256]{2,1,0:T(8,128)} %z_ref.5) | copy-start | bytes 5898244
  3.1 9.9 %copy-start.1 = (f32[30,64,256]{2,1,0:T(8,128)S(1)}, f32[30,64,256]{2,1,0:T(8,128)}, u32[]{:S(2)}) copy-start(f32[30,64,256]{2,1,0:T(8,128)} %z_ref.5) | copy-start | bytes 5898244
  3.2 15.7 %collective-permute-start.1 = (f32[32,256]{1,0:T(8,128)S(1)}, f32[32,256]{1,0:T(8,128)S(1)}, u32[]{:S(2)}, u32[]{:S(2)}) collective-permute-start(f32[32,256]{1,0:T(8,128)S(1)} %get-tuple-element.6.first_ref), channel_id=1, source_target_pairs={{8,0},{16,8},{24,16},{32,24},{40,32},{48,40},{56,48},{64,56},{72,6... | collective-permute-start | bytes 98312 | tf_op jit(solution)/shard_map/ppermute | solution.py:629
  11.0 7.9 %collective-permute-start = (f32[32,256]{1,0:T(8,128)S(1)}, f32[32,256]{1,0:T(8,128)S(1)}, u32[]{:S(2)}, u32[]{:S(2)}) collective-permute-start(f32[32,256]{1,0:T(8,128)S(1)} %get-tuple-element.7.last_ref), channel_id=1, source_target_pairs={{0,8},{8,16},{16,24},{24,32},{32,40},{40,48},{48,56},{56,64},{64,7... | collective-permute-start | bytes 98312 | tf_op jit(solution)/shard_map/ppermute | solution.py:628
  19.9 10.2 %all-to-all-start = ((f32[8,48,128]{2,1,0:T(8,128)}), f32[8,48,128]{2,1,0:T(8,128)S(1)}, u32[]{:S(2)}, u32[]{:S(2)}) async-start(f32[8,48,128]{2,1,0:T(8,128)} %rim.1), calls=%async_computation | async-start | bytes 393216 | tf_op jit(solution)/shard_map/all_to_all | solution.py:632

commit v3 on v2

--- a/solution.py
+++ b/solution.py
@@ -72,27 +72,30 @@
     tn = jnp.where(lane == ny - 1, 0.0, transmit(k, pltpu.roll(k, ny - 1, 1)))
     te = jnp.where(row == nx - 1, 0.0, transmit(k, pltpu.roll(k, nx - 1, 0)))
 
-    def apply(v, _):
-        z = z_ref[v]
-        fn = tn * (pltpu.roll(z, ny - 1, 1) - z)
-        fe = te * (pltpu.roll(z, nx - 1, 0) - z)
-        az_ref[v] = st * z - fn + pltpu.roll(fn, 1, 1) - fe + pltpu.roll(fe, 1, 0)
-        return 0
-
-    lax.fori_loop(0, vectors, apply, 0, unroll=6)
-    az_ref[vectors] = rs_ref[...]
-    az_ref[vectors + 1] = jnp.zeros((nx, ny), jnp.float32)
-
     groups = nx // 8
     pick_n, pick_c = iota((128, ny), 0), iota((128, ny), 1)
     edge_lane = jnp.where(((pick_n >> 3) & 1) == 0, 0, ny - 1)
+    ts = pltpu.roll(tn, 1, 1)
+    tw = pltpu.roll(te, 1, 0)
+    last_row, first_row = iota((8, ny), 0) == 7, iota((8, ny), 0) == 0
     gram, columns = None, None
     for g in range(groups):
-        rows = pl.ds(8 * g, 8)
-        zg = jnp.concatenate(
-            [z_ref[:, rows, :].reshape(8 * vectors, ny), k[8 * g : 8 * g + 8], jnp.zeros((8, ny), jnp.float32)], 0
-        )
-        ag = az_ref[:, rows, :].reshape(8 * (vectors + 2), ny)
+        at = slice(8 * g, 8 * g + 8)
+        tn_g, ts_g, te_g, tw_g, st_g = tn[at], ts[at], te[at], tw[at], st[at]
+        for v in range(vectors):
+            z = z_ref[v, at, :]
+            east = pltpu.roll(z, 7, 0)
+            if g + 1 < groups:
+                east = jnp.where(last_row, z_ref[v, 8 * g + 8 : 8 * g + 9, :], east)
+            west = pltpu.roll(z, 1, 0)
+            if g > 0:
+                west = jnp.where(first_row, z_ref[v, 8 * g - 1 : 8 * g, :], west)
+            near = tn_g * (z - pltpu.roll(z, ny - 1, 1)) + ts_g * (z - pltpu.roll(z, 1, 1))
+            az_ref[g % 2, v] = (st_g * z + te_g * (z - east)) + (tw_g * (z - west) + near)
+        az_ref[g % 2, vectors] = rs_ref[at, :]
+        az_ref[g % 2, vectors + 1] = jnp.zeros((8, ny), jnp.float32)
+        zg = jnp.concatenate([z_ref[:, at, :].reshape(8 * vectors, ny), k[at], jnp.zeros((8, ny), jnp.float32)], 0)
+        ag = az_ref[g % 2].reshape(8 * (vectors + 2), ny)
         zh, zm, zl = split_parts(zg)
         ah, am, al = split_parts(ag)
         left = jnp.concatenate([zh, zh, zm, zm, zh, zl], 1)
@@ -124,7 +127,7 @@
         out_shape=[f32(32, 128), f32(32, 128)],
         in_specs=[VMEM] * 4,
         out_specs=[VMEM, VMEM],
-        scratch_shapes=[pltpu.VMEM((vectors + 2, nx, ny), jnp.float32)],
+        scratch_shapes=[pltpu.VMEM((2, vectors + 2, 8, ny), jnp.float32)],
         compiler_params=limit(16),
         cost_estimate=pl.CostEstimate(flops=6 * 2 * 256 * 256 * 256 * 8, bytes_accessed=2 * 1024 * 1024, transcendentals=0),
         name="assemble",
@@ -192,9 +195,10 @@
     (inverse,) = invert_packed([jnp.where(diag, tile, 0.0) + jnp.where((lane >= NV) & (inner == row), 1.0, 0.0)])
     right_side = jnp.sum(jnp.where(lane == NV, tile, 0.0), 1, keepdims=True)
     right_row = jnp.sum(jnp.where(lane == row, jnp.broadcast_to(right_side, (32, 128)), 0.0), 0, keepdims=True)
-    even_diag = jnp.where(row < NV, inverse, jnp.where(row == NV, jnp.broadcast_to(right_row, (32, 128)), 0.0))
+    even_diag = jnp.where(row < NV, inverse, 0.0)
     before = pltpu.roll(tile, 96, 1)[:, :32]
     back = jnp.concatenate([jnp.transpose(before), jnp.zeros((32, 96), jnp.float32)], 1)
+    back = jnp.where(row == NV, jnp.broadcast_to(right_row, (32, 128)), back)
     even = jnp.where(lane < 32, back, jnp.where(lane < 32 + NV, pltpu.roll(even_diag, 32, 1), 0.0))
     odd = jnp.where(lane < 32, pltpu.roll(tile, 96, 1), jnp.where(lane < 64, pltpu.roll(tile, 32, 1), 0.0))
     both = jnp.where((place_ref[0] & 1) == 0, even, odd)
@@ -410,11 +414,7 @@
     def dot(a, b, dims=flat):
         return lax.dot_general(a, b, dims, preferred_element_type=jnp.float32)
 
-    def unpack(m):
-        t = all_ref[m]
-        return jnp.where((lanes & 32) == 0, jnp.concatenate([t, pltpu.roll(t, 96, 1)], 0), 0.0)
-
-    def for_all(total, body_fn, width=16):
+    def for_all(total, body_fn, width=32):
         if total <= width:
             for i in range(total):
                 body_fn(i)
@@ -428,30 +428,29 @@
             lax.fori_loop(0, total // width, step, 0)
 
     half = count // 2
-    index32 = inner
-    index_d = 64 + inner
+    inner16 = iota((16, 128), 1) & 31
+
+    def pick(t, top, bottom):
+        return jnp.concatenate([take(t, top + inner16), take(t, bottom + inner16)], 0)
+
+    second_64 = (lanes & 32) != 0
+    back_rows = second_64 & body
 
     def first_spread(j):
-        even, odd = unpack(2 * j), unpack(2 * j + 1)
-        inverse = take(even, index_d)
-        back = take(even, index32)
-        ahead = take(odd, index32)
-        right_row = jnp.broadcast_to(inverse[NV : NV + 1], (32, 128))
-        left = six_left(jnp.where(body, inverse, 0.0), lanes)
-        tb, ta, tr = six_right(back, lanes), six_right(ahead, lanes), six_right(right_row, lanes)
-        is_r = iota((32, 192), 0) == NV
+        even, odd = all_ref[2 * j], all_ref[2 * j + 1]
+        inverse = pick(even, 64, 96)
+        back = pick(even, 0, 32)
+        ahead = pick(odd, 0, 32)
+        left = six_left(inverse, lanes)
+        tb = six_right(back, lanes)
+        ta = six_right(jnp.where(rows == NV, jnp.broadcast_to(back[NV : NV + 1], (32, 128)), ahead), lanes)
         zero = jnp.zeros((32, 192), jnp.bfloat16)
-
-        def with_r(t):
-            return jnp.where(is_r, tr.astype(jnp.float32), t.astype(jnp.float32)).astype(jnp.bfloat16)
-
-        right = jnp.concatenate([tb, zero, with_r(ta), zero, zero, ta, with_r(tb), zero], 0)
-        x = dot(left, right, NT)
+        x = dot(left, jnp.concatenate([tb, zero, ta, zero, zero, ta, tb, zero], 0), NT)
         xa[j] = x[:, :128]
         xb[j] = x[:, 128:]
-        aug[j] = odd
-        coupling[j] = jnp.where((lanes & 63) < 32, ahead, 0.0)
-        coupling[count + j] = jnp.where((lanes & 63) < 32, 0.0, back)
+        aug[j] = jnp.concatenate([odd, pltpu.roll(odd, 96, 1)], 0)
+        coupling[j] = jnp.where(second_64, 0.0, ahead)
+        coupling[count + j] = jnp.where(back_rows, back, 0.0)
 
     for_all(half, first_spread)
     xb[half] = blank

time: 80.2 us -> 76.3 us (0.951)
  Pallas kernels: 23.9 us -> 20 us
    pallas_call x1, Pallas kernels: 5.88 us -> 3.72 us  [assemble(): pl.pallas_call(assemble_kernel, out_shape=[f32(32, 128), f32(32, 128)], i...]
    pallas_call x1, Pallas kernels: 15.2 us -> 13.4 us  [solve(): pl.pallas_call(functools.partial(solve_kernel, count), out_shape=[f32(1,...]
  transfers between devices with their start and end apart: 3 -> 3, of which waited for: 1 -> 2; matrix products, arithmetic and copies ran while one was open for 0% -> 0% of each run, Pallas kernels for 7% -> 5%
where the time goes in v3:
time: 76.3 us; the launch traced here: 75.9 us
  blocking collectives  32.7 us (43%)
  Pallas kernels  20 us (26%)
  starting transfers between devices  13.2 us (17%)
  waiting for transfers between devices  6.79 us (9%)
  local copies, waits for them, and re-layouts  1.55 us (2%)
  other arithmetic  1 us (1%)
    all_to_all x1, blocking collectives, per_device(): gathered = lax.all_to_all(total(place, g, subs), 'sub', 0, 0)  32.7 us
    pallas_call x1, Pallas kernels, solve(): pl.pallas_call(functools.partial(solve_kernel, count), out_shape=[f32(1,...  13.4 us
    ppermute x1, starting transfers between devices, per_device(): down = lax.ppermute(first, 'sub', [(j, i) for i, j in ahead])  7.86 us
    all_to_all x1, waiting for transfers between devices, per_device(): g = lax.all_to_all(share, 'own', 0, 0)  6.67 us
    pallas_call x1, Pallas kernels, assemble(): pl.pallas_call(assemble_kernel, out_shape=[f32(32, 128), f32(32, 128)], i...  3.72 us
    all_to_all x1, starting transfers between devices, per_device(): g = lax.all_to_all(share, 'own', 0, 0)  3.39 us
    ppermute x1, starting transfers between devices, per_device(): up = lax.ppermute(last, 'sub', ahead)  1.92 us
    pallas_call x1, Pallas kernels, total(): pl.pallas_call(total_kernel, out_shape=f32(copies, 16, 128), in_specs=[SM...  1.85 us
  transfers between devices with their start and end apart: 3, of which 2 were waited for; matrix products, arithmetic and copies ran while one was open for 0% of the time, Pallas kernels for 5%

profile of v3, /device:TPU:8, one launch (start us, length us, event | category | flops | bytes accessed | tf_op | source)
XLA Modules:
  0.0 75.9 jit_solution(18228482231896396188)
XLA Ops:
  0.6 0.0 copy-start.3
  0.6 0.0 copy-start.2
  0.7 0.9 %exponential_multiply_fusion.k_ref = f32[64,256]{1,0:T(8,128)S(1)} fusion(f32[64,256]{1,0:T(8,128)} %param.6, s32[64,256]{1,0:T(8,128)} %param.7), kind=kLoop, calls=%fused_computation | loop fusion | flops 65536 | bytes 196608 | tf_op jit(solution)/shard_map/mul | solution.py:32
  1.6 0.0 copy-start
  1.6 1.5 %copy-done = f32[30,64,256]{2,1,0:T(8,128)S(1)} copy-done((f32[30,64,256]{2,1,0:T(8,128)S(1)}, f32[30,64,256]{2,1,0:T(8,128)}, u32[]{:S(2)}) %copy-start) | copy-done | bytes 1966104
  3.1 0.0 copy-start.1
  3.2 7.9 %collective-permute-start.1 = (f32[32,256]{1,0:T(8,128)S(1)}, f32[32,256]{1,0:T(8,128)S(1)}, u32[]{:S(2)}, u32[]{:S(2)}) collective-permute-start(f32[32,256]{1,0:T(8,128)S(1)} %get-tuple-element.6.first_ref), channel_id=1, source_target_pairs={{8,0},{16,8},{24,16},{32,24},{40,32},{48,40},{56,48},{64,56},{72,6... | collective-permute-start | bytes 98312 | tf_op jit(solution)/shard_map/ppermute | solution.py:628
  11.0 1.9 %collective-permute-start = (f32[32,256]{1,0:T(8,128)S(1)}, f32[32,256]{1,0:T(8,128)S(1)}, u32[]{:S(2)}, u32[]{:S(2)}) collective-permute-start(f32[32,256]{1,0:T(8,128)S(1)} %get-tuple-element.7.last_ref), channel_id=1, source_target_pairs={{0,8},{8,16},{16,24},{24,32},{32,40},{40,48},{48,56},{56,64},{64,7... | collective-permute-start | bytes 98312 | tf_op jit(solution)/shard_map/ppermute | solution.py:627
  13.0 0.0 copy-done.3
  13.0 0.0 copy-done.2
  13.0 0.0 copy-done.1
  13.0 3.7 %assemble.1 = (f32[32,128]{1,0:T(8,128)S(1)}, f32[32,128]{1,0:T(8,128)S(1)}) custom-call(f32[30,64,256]{2,1,0:T(8,128)S(1)} %copy-done.1, f32[64,256]{1,0:T(8,128)S(1)} %exponential_multiply_fusion.k_ref, f32[64,256]{1,0:T(8,128)S(1)} %copy-done.2, f32[64,256]{1,0:T(8,128)S(1)} %copy-done.3), custom_call_target="tpu_custom_call" | custom-call | flops 1610612736 | bytes 2097152 | tf_op jit(solution)/shard_map/assemble/pallas_call | solution.py:125
  16.7 0.0 collective-permute-done.1.down_ref
  16.7 0.1 collective-permute-done.up_ref
  16.8 1.0 %rim.1 = f32[8,48,128]{2,1,0:T(8,128)} custom-call(f32[32,256]{1,0:T(8,128)S(1)} %get-tuple-element.6.first_ref, f32[32,256]{1,0:T(8,128)S(1)} %get-tuple-element.7.last_ref, f32[32,256]{1,0:T(8,128)S(1)} %collective-permute-done.up_ref, f32[32,256]{1,0:T(8,128)S(1)} %collective-permute-done.1.down_ref, f32[32,128]{1,0:T(8,128)S(1)} %get-tuple-element.8.p_ref, ...), custom_call_target="tpu_custom_call" | custom-call | tf_op jit(solution)/shard_map/rim/pallas_call | solution.py:162
  17.8 3.4 %all-to-all-start = ((f32[8,48,128]{2,1,0:T(8,128)}), f32[8,48,128]{2,1,0:T(8,128)S(1)}, u32[]{:S(2)}, u32[]{:S(2)}) async-start(f32[8,48,128]{2,1,0:T(8,128)} %rim.1), calls=%async_computation | async-start | bytes 393216 | tf_op jit(solution)/shard_map/all_to_all | solution.py:631
  21.2 0.1 pad_add_fusion.place_ref
  21.3 6.7 %all-to-all-done.g_ref = f32[8,48,128]{2,1,0:T(8,128)S(1)} async-done(((f32[8,48,128]{2,1,0:T(8,128)}), f32[8,48,128]{2,1,0:T(8,128)S(1)}, u32[]{:S(2)}, u32[]{:S(2)}) %all-to-all-start) | async-done | bytes 196640 | tf_op jit(solution)/shard_map/all_to_all | solution.py:631
  28.0 1.9 %total.1 = f32[64,16,128]{2,1,0:T(8,128)S(1)} custom-call(s32[2]{0:T(128)S(1)} %pad_add_fusion.place_ref, f32[8,48,128]{2,1,0:T(8,128)S(1)} %all-to-all-done.g_ref), custom_call_target="tpu_custom_call" | custom-call | tf_op jit(solution)/shard_map/total/pallas_call | solution.py:217
  29.8 32.7 %all_to_all.10.all_ref = f32[64,16,128]{2,1,0:T(8,128)S(1)} all-to-all(f32[64,16,128]{2,1,0:T(8,128)S(1)} %total.1), channel_id=1, replica_groups=mesh['sub'=64,'own'=8] {'sub'}, dimensions={0} | all-to-all | bytes 1048576 | tf_op jit(solution)/shard_map/all_to_all | solution.py:632
  62.5 13.4 %solve.1 = (f32[1,30]{1,0:T(1,128)}, f32[64,256]{1,0:T(8,128)}) custom-call(s32[2]{0:T(128)S(1)} %pad_add_fusion.place_ref, f32[64,16,128]{2,1,0:T(8,128)S(1)} %all_to_all.10.all_ref, f32[30,64,256]{2,1,0:T(8,128)S(1)} %copy-done.1, f32[64,256]{1,0:T(8,128)S(1)} %exponential_multiply_fusion.k_ref, f32[64,256]{1,0:T(8,128)S(1)} %copy-done.2, ...), custom_call_target="tpu_custom_call" | custom-call | tf_op jit(solution)/shard_map/solve/pallas_call | solution.py:610
  (1 shorter events, 0.0 us)
Async XLA Ops:
  0.6 12.3 %copy-start.3 = (f32[64,256]{1,0:T(8,128)S(1)}, f32[64,256]{1,0:T(8,128)}, u32[]{:S(2)}) copy-start(f32[64,256]{1,0:T(8,128)} %rs_ref.3) | copy-start | bytes 196612
  0.6 12.3 %copy-start.2 = (f32[64,256]{1,0:T(8,128)S(1)}, f32[64,256]{1,0:T(8,128)}, u32[]{:S(2)}) copy-start(f32[64,256]{1,0:T(8,128)} %st_ref.3) | copy-start | bytes 196612
  1.6 1.5 %copy-start = (f32[30,64,256]{2,1,0:T(8,128)S(1)}, f32[30,64,256]{2,1,0:T(8,128)}, u32[]{:S(2)}) copy-start(f32[30,64,256]{2,1,0:T(8,128)} %z_ref.5) | copy-start | bytes 5898244
  3.1 9.9 %copy-start.1 = (f32[30,64,256]{2,1,0:T(8,128)S(1)}, f32[30,64,256]{2,1,0:T(8,128)}, u32[]{:S(2)}) copy-start(f32[30,64,256]{2,1,0:T(8,128)} %z_ref.5) | copy-start | bytes 5898244
  3.2 13.6 %collective-permute-start.1 = (f32[32,256]{1,0:T(8,128)S(1)}, f32[32,256]{1,0:T(8,128)S(1)}, u32[]{:S(2)}, u32[]{:S(2)}) collective-permute-start(f32[32,256]{1,0:T(8,128)S(1)} %get-tuple-element.6.first_ref), channel_id=1, source_target_pairs={{8,0},{16,8},{24,16},{32,24},{40,32},{48,40},{56,48},{64,56},{72,6... | collective-permute-start | bytes 98312 | tf_op jit(solution)/shard_map/ppermute | solution.py:628
  11.0 5.8 %collective-permute-start = (f32[32,256]{1,0:T(8,128)S(1)}, f32[32,256]{1,0:T(8,128)S(1)}, u32[]{:S(2)}, u32[]{:S(2)}) collective-permute-start(f32[32,256]{1,0:T(8,128)S(1)} %get-tuple-element.7.last_ref), channel_id=1, source_target_pairs={{0,8},{8,16},{16,24},{24,32},{32,40},{40,48},{48,56},{56,64},{64,7... | collective-permute-start | bytes 98312 | tf_op jit(solution)/shard_map/ppermute | solution.py:627
  17.8 10.2 %all-to-all-start = ((f32[8,48,128]{2,1,0:T(8,128)}), f32[8,48,128]{2,1,0:T(8,128)S(1)}, u32[]{:S(2)}, u32[]{:S(2)}) async-start(f32[8,48,128]{2,1,0:T(8,128)} %rim.1), calls=%async_computation | async-start | bytes 393216 | tf_op jit(solution)/shard_map/all_to_all | solution.py:631

commit v4 on v3

--- a/solution.py
+++ b/solution.py
@@ -44,24 +44,30 @@
     return high, middle, low
 
 
-def edges_kernel(z_ref, k_ref, first_ref, last_ref):
+def edges_kernel(z_ref, k_ref, out_ref):
     vectors, nx, ny = z_ref.shape
     pad = jnp.zeros((31 - vectors, ny), jnp.float32)
-    for row, out in ((0, first_ref), (nx - 1, last_ref)):
+    for row, at in ((0, 0), (nx - 1, 32)):
         rows = [z_ref[v, row : row + 1, :] for v in range(vectors)]
-        out[...] = jnp.concatenate(rows + [k_ref[row : row + 1, :], pad], 0)
+        out_ref[at : at + 32, :] = jnp.concatenate(rows + [k_ref[row : row + 1, :], pad], 0)
 
 
 def edges(z, k):
-    ny = k.shape[1]
     return pl.pallas_call(
         edges_kernel,
-        out_shape=[f32(32, ny), f32(32, ny)],
+        out_shape=f32(64, k.shape[1]),
         in_specs=[VMEM, VMEM],
-        out_specs=[VMEM, VMEM],
+        out_specs=VMEM,
         compiler_params=limit(4),
         name="edges",
     )(z, k)
+
+
+def neighbours(place_ref, a_ref, b_ref):
+    odd = (place_ref[0] & 1) == 1
+    up = jnp.where(odd, a_ref[32:, :], b_ref[32:, :])
+    down = jnp.where(odd, b_ref[:32, :], a_ref[:32, :])
+    return up, down
 
 
 def assemble_kernel(z_ref, k_ref, st_ref, rs_ref, p_ref, c_ref, az_ref):
@@ -139,14 +145,15 @@
     return jnp.where(lane < 64, tile[:16], pltpu.roll(tile[16:], 64, 1))
 
 
-def rim_kernel(first_ref, last_ref, up_ref, down_ref, p_ref, c_ref, out_ref):
-    ny = first_ref.shape[1]
+def rim_kernel(place_ref, edge_ref, a_ref, b_ref, p_ref, c_ref, out_ref):
+    ny = edge_ref.shape[1]
     body = iota((32, ny), 0) < NV
-    tw = transmit(first_ref[NV : NV + 1], up_ref[NV : NV + 1])
-    te = transmit(last_ref[NV : NV + 1], down_ref[NV : NV + 1])
-    first = jnp.where(body, first_ref[...], 0.0)
-    last = jnp.where(body, last_ref[...], 0.0)
-    above = jnp.where(body, up_ref[...], 0.0)
+    up, down = neighbours(place_ref, a_ref, b_ref)
+    tw = transmit(edge_ref[NV : NV + 1, :], up[NV : NV + 1])
+    te = transmit(edge_ref[32 + NV : 33 + NV, :], down[NV : NV + 1])
+    first = jnp.where(body, edge_ref[:32, :], 0.0)
+    last = jnp.where(body, edge_ref[32:, :], 0.0)
+    above = jnp.where(body, up, 0.0)
     blank = jnp.zeros((32, ny), jnp.float32)
     left = jnp.concatenate([first * tw, last * te], 1)
     right = jnp.concatenate(
@@ -158,15 +165,15 @@
         out_ref[o] = share
 
 
-def rim(first, last, up, down, p, c, copies):
+def rim(place, edge, a, b, p, c, copies):
     return pl.pallas_call(
         rim_kernel,
         out_shape=f32(copies, 48, 128),
-        in_specs=[VMEM] * 6,
+        in_specs=[SMEM] + [VMEM] * 5,
         out_specs=VMEM,
         compiler_params=limit(4),
         name="rim",
-    )(first, last, up, down, p, c)
+    )(place, edge, a, b, p, c)
 
 
 def total_kernel(place_ref, g_ref, out_ref):
@@ -390,8 +397,8 @@
     k_ref,
     st_ref,
     rs_ref,
-    up_ref,
-    down_ref,
+    a_ref,
+    b_ref,
     g_ref,
     coeff_ref,
     out_ref,
@@ -549,10 +556,10 @@
             jnp.where(odd, eb, window[1]),
         ]
     coeff_ref[...] = window[1][0:1, :NV]
-    finish(place_ref, window, z_ref, k_ref, st_ref, rs_ref, up_ref, down_ref, g_ref, out_ref)
-
-
-def finish(place_ref, window, z_ref, k_ref, st_ref, rs_ref, up_ref, down_ref, g_ref, out_ref):
+    finish(place_ref, window, z_ref, k_ref, st_ref, rs_ref, a_ref, b_ref, g_ref, out_ref)
+
+
+def finish(place_ref, window, z_ref, k_ref, st_ref, rs_ref, a_ref, b_ref, g_ref, out_ref):
     vectors, nx, ny = z_ref.shape
     own, owners = place_ref[1], g_ref.shape[0]
     lane8 = iota((8, 128), 1)
@@ -570,9 +577,10 @@
         return jnp.dot(row[:, :32], block, precision=precise, preferred_element_type=jnp.float32)
 
     body = iota((32, ny), 0) < NV
-    f_up = in_row(window[0], jnp.where(body, up_ref[...], 0.0))[0:1]
-    f_down = in_row(window[2], jnp.where(body, down_ref[...], 0.0))[0:1]
-    k_up, k_down = up_ref[NV : NV + 1], down_ref[NV : NV + 1]
+    up, down = neighbours(place_ref, a_ref, b_ref)
+    f_up = in_row(window[0], jnp.where(body, up, 0.0))[0:1]
+    f_down = in_row(window[2], jnp.where(body, down, 0.0))[0:1]
+    k_up, k_down = up[NV : NV + 1], down[NV : NV + 1]
 
     def beside(o, side, there):
         block = g_ref[o, 16:48, :]
@@ -604,7 +612,7 @@
     out_ref[...] = rs_ref[...] - applied
 
 
-def solve(place, gathered, z, k, st, rs, up, down, g):
+def solve(place, gathered, z, k, st, rs, a, b, g):
     count = gathered.shape[0]
     nx, ny = k.shape
     return pl.pallas_call(
@@ -615,22 +623,23 @@
         scratch_shapes=[pltpu.VMEM((n, 32, 128), jnp.float32) for n in (count // 2, count, count + 1, 2 * count)],
         compiler_params=limit(16),
         name="solve",
-    )(place, gathered, z, k, st, rs, up, down, g)
+    )(place, gathered, z, k, st, rs, a, b, g)
 
 
 def per_device(deflation, permeability_base, design_mask, storage, right_side):
     subs, owners = lax.axis_size("sub"), lax.axis_size("own")
     place = jnp.stack([lax.axis_index("sub"), lax.axis_index("own")]).astype(jnp.int32)
     k = permeability(permeability_base, design_mask)
-    first, last = edges(deflation, k)
-    ahead = [(i, i + 1) for i in range(subs - 1)]
-    up = lax.ppermute(last, "sub", ahead)
-    down = lax.ppermute(first, "sub", [(j, i) for i, j in ahead])
+    edge = edges(deflation, k)
+    swaps = [(i, i ^ 1) for i in range(subs) if i ^ 1 < subs]
+    others = [(i, i + 1 if i % 2 else i - 1) for i in range(1, subs) if i % 2 == 0 or i + 1 < subs]
+    a = lax.ppermute(edge, "sub", swaps)
+    b = lax.ppermute(edge, "sub", others)
     p, c = assemble(deflation, k, storage, right_side)
-    share = rim(first, last, up, down, p, c, owners)
+    share = rim(place, edge, a, b, p, c, owners)
     g = lax.all_to_all(share, "own", 0, 0)
     gathered = lax.all_to_all(total(place, g, subs), "sub", 0, 0)
-    return tuple(solve(place, gathered, deflation, k, storage, right_side, up, down, g))
+    return tuple(solve(place, gathered, deflation, k, storage, right_side, a, b, g))
 
 
 def solution(mesh):

time: 76.3 us -> 75.3 us (0.987)
  blocking collectives: 32.7 us -> 43.3 us
  waiting for transfers between devices: 6.79 us -> 0.01 us
  starting transfers between devices: 13.2 us -> 8.53 us
    all_to_all x0 -> x1, blocking collectives: none -> 9.23 us  [per_device(): g = lax.all_to_all(share, 'own', 0, 0)]
    all_to_all x1 -> x0, waiting for transfers between devices: 6.67 us -> none  [per_device(): g = lax.all_to_all(share, 'own', 0, 0)]
    all_to_all x1 -> x0, starting transfers between devices: 3.39 us -> none  [per_device(): g = lax.all_to_all(share, 'own', 0, 0)]
    all_to_all x1, blocking collectives: 32.7 us -> 34.1 us  [per_device(): gathered = lax.all_to_all(total(place, g, subs), 'sub', 0, 0)]
    ppermute x2, starting transfers between devices: 9.78 us -> 8.53 us  [the longest x1 4.91 us: per_device(): a = lax.ppermute(edge, 'sub', swaps)]
  transfers between devices with their start and end apart: 3 -> 2, of which waited for: 2 -> 0; matrix products, arithmetic and copies ran while one was open for 0% -> 0% of each run, Pallas kernels for 5% -> 5%
where the time goes in v4:
time: 75.3 us; the launch traced here: 75 us
  blocking collectives  43.3 us (58%)
  Pallas kernels  19.9 us (26%)
  starting transfers between devices  8.53 us (11%)
  local copies, waits for them, and re-layouts  1.55 us (2%)
  other arithmetic  1.01 us (1%)
    all_to_all x1, blocking collectives, per_device(): gathered = lax.all_to_all(total(place, g, subs), 'sub', 0, 0)  34.1 us
    pallas_call x1, Pallas kernels, solve(): pl.pallas_call(functools.partial(solve_kernel, count), out_shape=[f32(1,...  13.4 us
    all_to_all x1, blocking collectives, per_device(): g = lax.all_to_all(share, 'own', 0, 0)  9.23 us
    ppermute x1, starting transfers between devices, per_device(): a = lax.ppermute(edge, 'sub', swaps)  4.91 us
    pallas_call x1, Pallas kernels, assemble(): pl.pallas_call(assemble_kernel, out_shape=[f32(32, 128), f32(32, 128)], i...  3.72 us
    ppermute x1, starting transfers between devices, per_device(): b = lax.ppermute(edge, 'sub', others)  3.62 us
    pallas_call x1, Pallas kernels, total(): pl.pallas_call(total_kernel, out_shape=f32(copies, 16, 128), in_specs=[SM...  1.86 us
    unnamed x8, local copies, waits for them, and re-layouts  1.55 us
  transfers between devices with their start and end apart: 2, of which 0 were waited for; matrix products, arithmetic and copies ran while one was open for 0% of the time, Pallas kernels for 5%

profile of v4, /device:TPU:8, one launch (start us, length us, event | category | flops | bytes accessed | tf_op | source)
XLA Modules:
  0.0 75.0 jit_solution(5852983025615636436)
XLA Ops:
  0.6 0.0 copy-start.3
  0.6 0.0 copy-start.2
  0.7 0.9 %exponential_multiply_fusion.k_ref = f32[64,256]{1,0:T(8,128)S(1)} fusion(f32[64,256]{1,0:T(8,128)} %param.6, s32[64,256]{1,0:T(8,128)} %param.7), kind=kLoop, calls=%fused_computation | loop fusion | flops 65536 | bytes 196608 | tf_op jit(solution)/shard_map/mul | solution.py:32
  1.6 0.0 copy-start
  1.6 1.5 %copy-done = f32[30,64,256]{2,1,0:T(8,128)S(1)} copy-done((f32[30,64,256]{2,1,0:T(8,128)S(1)}, f32[30,64,256]{2,1,0:T(8,128)}, u32[]{:S(2)}) %copy-start) | copy-done | bytes 1966104
  3.1 0.0 copy-start.1
  3.2 3.6 %collective-permute-start.1 = (f32[64,256]{1,0:T(8,128)S(1)}, f32[64,256]{1,0:T(8,128)S(1)}, u32[]{:S(2)}, u32[]{:S(2)}) collective-permute-start(f32[64,256]{1,0:T(8,128)S(1)} %edges.1.edge_ref), channel_id=1, source_target_pairs={{8,16},{16,8},{24,32},{32,24},{40,48},{48,40},{56,64},{64,56},{72,... | collective-permute-start | bytes 196616 | tf_op jit(solution)/shard_map/ppermute | solution.py:637
  6.8 4.9 %collective-permute-start = (f32[64,256]{1,0:T(8,128)S(1)}, f32[64,256]{1,0:T(8,128)S(1)}, u32[]{:S(2)}, u32[]{:S(2)}) collective-permute-start(f32[64,256]{1,0:T(8,128)S(1)} %edges.1.edge_ref), channel_id=1, source_target_pairs={{0,8},{8,0},{16,24},{24,16},{32,40},{40,32},{48,56},{56,48},{64,72... | collective-permute-start | bytes 196616 | tf_op jit(solution)/shard_map/ppermute | solution.py:636
  11.7 0.0 copy-done.3
  11.7 0.0 copy-done.2
  11.7 0.0 copy-done.1
  11.7 3.7 %assemble.1 = (f32[32,128]{1,0:T(8,128)S(1)}, f32[32,128]{1,0:T(8,128)S(1)}) custom-call(f32[30,64,256]{2,1,0:T(8,128)S(1)} %copy-done.1, f32[64,256]{1,0:T(8,128)S(1)} %exponential_multiply_fusion.k_ref, f32[64,256]{1,0:T(8,128)S(1)} %copy-done.2, f32[64,256]{1,0:T(8,128)S(1)} %copy-done.3), custom_call_target="tpu_custom_call" | custom-call | flops 1610612736 | bytes 2097152 | tf_op jit(solution)/shard_map/assemble/pallas_call | solution.py:131
  15.5 0.1 pad_add_fusion.place_ref
  15.6 0.0 collective-permute-done.1.b_ref
  15.6 0.0 collective-permute-done.a_ref
  15.6 0.8 %rim.1 = f32[8,48,128]{2,1,0:T(8,128)S(1)} custom-call(s32[2]{0:T(128)S(1)} %pad_add_fusion.place_ref, f32[64,256]{1,0:T(8,128)S(1)} %edges.1.edge_ref, f32[64,256]{1,0:T(8,128)S(1)} %collective-permute-done.a_ref, f32[64,256]{1,0:T(8,128)S(1)} %collective-permute-done.1.b_ref, f32[32,128]{1,0:T(8,128)S(1)} %get-tuple-element.4.p_ref, ...), custom_call_target="tpu_custom_call" | custom-call | tf_op jit(solution)/shard_map/rim/pallas_call | solution.py:169
  16.4 9.2 %all_to_all.10.g_ref = f32[8,48,128]{2,1,0:T(8,128)S(1)} all-to-all(f32[8,48,128]{2,1,0:T(8,128)S(1)} %rim.1), channel_id=1, replica_groups=mesh['sub'=64,'own'=8] {'own'}, dimensions={0} | all-to-all | bytes 393216 | tf_op jit(solution)/shard_map/all_to_all | solution.py:640
  25.6 1.9 %total.1 = f32[64,16,128]{2,1,0:T(8,128)S(1)} custom-call(s32[2]{0:T(128)S(1)} %pad_add_fusion.place_ref, f32[8,48,128]{2,1,0:T(8,128)S(1)} %all_to_all.10.g_ref), custom_call_target="tpu_custom_call" | custom-call | tf_op jit(solution)/shard_map/total/pallas_call | solution.py:224
  27.5 34.1 %all_to_all.11.all_ref = f32[64,16,128]{2,1,0:T(8,128)S(1)} all-to-all(f32[64,16,128]{2,1,0:T(8,128)S(1)} %total.1), channel_id=1, replica_groups=mesh['sub'=64,'own'=8] {'sub'}, dimensions={0} | all-to-all | bytes 1048576 | tf_op jit(solution)/shard_map/all_to_all | solution.py:641
  61.5 13.4 %solve.1 = (f32[1,30]{1,0:T(1,128)}, f32[64,256]{1,0:T(8,128)}) custom-call(s32[2]{0:T(128)S(1)} %pad_add_fusion.place_ref, f32[64,16,128]{2,1,0:T(8,128)S(1)} %all_to_all.11.all_ref, f32[30,64,256]{2,1,0:T(8,128)S(1)} %copy-done.1, f32[64,256]{1,0:T(8,128)S(1)} %exponential_multiply_fusion.k_ref, f32[64,256]{1,0:T(8,128)S(1)} %copy-done.2, ...), custom_call_target="tpu_custom_call" | custom-call | tf_op jit(solution)/shard_map/solve/pallas_call | solution.py:618
  (1 shorter events, 0.0 us)
Async XLA Ops:
  0.6 11.1 %copy-start.3 = (f32[64,256]{1,0:T(8,128)S(1)}, f32[64,256]{1,0:T(8,128)}, u32[]{:S(2)}) copy-start(f32[64,256]{1,0:T(8,128)} %rs_ref.3) | copy-start | bytes 196612
  0.6 11.1 %copy-start.2 = (f32[64,256]{1,0:T(8,128)S(1)}, f32[64,256]{1,0:T(8,128)}, u32[]{:S(2)}) copy-start(f32[64,256]{1,0:T(8,128)} %st_ref.3) | copy-start | bytes 196612
  1.6 1.5 %copy-start = (f32[30,64,256]{2,1,0:T(8,128)S(1)}, f32[30,64,256]{2,1,0:T(8,128)}, u32[]{:S(2)}) copy-start(f32[30,64,256]{2,1,0:T(8,128)} %z_ref.5) | copy-start | bytes 5898244
  3.1 8.6 %copy-start.1 = (f32[30,64,256]{2,1,0:T(8,128)S(1)}, f32[30,64,256]{2,1,0:T(8,128)}, u32[]{:S(2)}) copy-start(f32[30,64,256]{2,1,0:T(8,128)} %z_ref.5) | copy-start | bytes 5898244
  3.2 12.4 %collective-permute-start.1 = (f32[64,256]{1,0:T(8,128)S(1)}, f32[64,256]{1,0:T(8,128)S(1)}, u32[]{:S(2)}, u32[]{:S(2)}) collective-permute-start(f32[64,256]{1,0:T(8,128)S(1)} %edges.1.edge_ref), channel_id=1, source_target_pairs={{8,16},{16,8},{24,32},{32,24},{40,48},{48,40},{56,64},{64,56},{72,... | collective-permute-start | bytes 196616 | tf_op jit(solution)/shard_map/ppermute | solution.py:637
  6.8 8.8 %collective-permute-start = (f32[64,256]{1,0:T(8,128)S(1)}, f32[64,256]{1,0:T(8,128)S(1)}, u32[]{:S(2)}, u32[]{:S(2)}) collective-permute-start(f32[64,256]{1,0:T(8,128)S(1)} %edges.1.edge_ref), channel_id=1, source_target_pairs={{0,8},{8,0},{16,24},{24,16},{32,40},{40,32},{48,56},{56,48},{64,72... | collective-permute-start | bytes 196616 | tf_op jit(solution)/shard_map/ppermute | solution.py:636

commit v5 on v4

--- a/solution.py
+++ b/solution.py
@@ -216,14 +216,15 @@
         top,
         jnp.where(half < 64, pltpu.roll(bottom, 32, 1), jnp.where(half < 96, pltpu.roll(top, 32, 1), pltpu.roll(bottom, 64, 1))),
     )
+    share = jnp.where((place_ref[1] & 1) == 0, packed[:8], packed[8:])
     for s in range(out_ref.shape[0]):
-        out_ref[s] = packed
+        out_ref[s] = share
 
 
 def total(place, g, copies):
     return pl.pallas_call(
         total_kernel,
-        out_shape=f32(copies, 16, 128),
+        out_shape=f32(copies, 8, 128),
         in_specs=[SMEM, VMEM],
         out_specs=VMEM,
         compiler_params=limit(4),
@@ -392,7 +393,8 @@
 def solve_kernel(
     count,
     place_ref,
-    all_ref,
+    mine_ref,
+    other_ref,
     z_ref,
     k_ref,
     st_ref,
@@ -443,8 +445,14 @@
     second_64 = (lanes & 32) != 0
     back_rows = second_64 & body
 
+    first_core = (place_ref[1] & 1) == 0
+
+    def block(m):
+        mine, other = mine_ref[m], other_ref[m]
+        return jnp.concatenate([jnp.where(first_core, mine, other), jnp.where(first_core, other, mine)], 0)
+
     def first_spread(j):
-        even, odd = all_ref[2 * j], all_ref[2 * j + 1]
+        even, odd = block(2 * j), block(2 * j + 1)
         inverse = pick(even, 64, 96)
         back = pick(even, 0, 32)
         ahead = pick(odd, 0, 32)
@@ -612,18 +620,18 @@
     out_ref[...] = rs_ref[...] - applied
 
 
-def solve(place, gathered, z, k, st, rs, a, b, g):
-    count = gathered.shape[0]
+def solve(place, mine, other, z, k, st, rs, a, b, g):
+    count = mine.shape[0]
     nx, ny = k.shape
     return pl.pallas_call(
         functools.partial(solve_kernel, count),
         out_shape=[f32(1, NV), f32(nx, ny)],
-        in_specs=[SMEM] + [VMEM] * 8,
+        in_specs=[SMEM] + [VMEM] * 9,
         out_specs=[VMEM, VMEM],
         scratch_shapes=[pltpu.VMEM((n, 32, 128), jnp.float32) for n in (count // 2, count, count + 1, 2 * count)],
         compiler_params=limit(16),
         name="solve",
-    )(place, gathered, z, k, st, rs, a, b, g)
+    )(place, mine, other, z, k, st, rs, a, b, g)
 
 
 def per_device(deflation, permeability_base, design_mask, storage, right_side):
@@ -638,8 +646,9 @@
     p, c = assemble(deflation, k, storage, right_side)
     share = rim(place, edge, a, b, p, c, owners)
     g = lax.all_to_all(share, "own", 0, 0)
-    gathered = lax.all_to_all(total(place, g, subs), "sub", 0, 0)
-    return tuple(solve(place, gathered, deflation, k, storage, right_side, a, b, g))
+    mine = lax.all_to_all(total(place, g, subs), "sub", 0, 0)
+    other = lax.ppermute(mine, "own", [(i, i ^ 1) for i in range(owners)])
+    return tuple(solve(place, mine, other, deflation, k, storage, right_side, a, b, g))
 
 
 def solution(mesh):

time: 75.3 us -> 75.4 us (level)
  the two profiles are of different devices: /device:TPU:8 before, /device:TPU:1 now
where the time goes in v5:
time: 75.4 us; the launch traced here: 75 us
  blocking collectives  38 us (50%)
  Pallas kernels  19.9 us (26%)
  starting transfers between devices  12.9 us (17%)
  local copies, waits for them, and re-layouts  1.55 us (2%)
  other arithmetic  1.01 us (1%)
  waiting for transfers between devices  0.96 us (1%)
    all_to_all x1, blocking collectives, per_device(): mine = lax.all_to_all(total(place, g, subs), 'sub', 0, 0)  26.8 us
    pallas_call x1, Pallas kernels, solve(): pl.pallas_call(functools.partial(solve_kernel, count), out_shape=[f32(1,...  13.5 us
    all_to_all x1, blocking collectives, per_device(): g = lax.all_to_all(share, 'own', 0, 0)  11.2 us
    ppermute x1, starting transfers between devices, per_device(): a = lax.ppermute(edge, 'sub', swaps)  6.57 us
    ppermute x1, starting transfers between devices, per_device(): other = lax.ppermute(mine, 'own', [(i, i ^ 1) for i in range(owners)])  5.55 us
    pallas_call x1, Pallas kernels, assemble(): pl.pallas_call(assemble_kernel, out_shape=[f32(32, 128), f32(32, 128)], i...  3.72 us
    pallas_call x1, Pallas kernels, total(): pl.pallas_call(total_kernel, out_shape=f32(copies, 8, 128), in_specs=[SME...  1.84 us
    unnamed x8, local copies, waits for them, and re-layouts  1.55 us
  transfers between devices with their start and end apart: 3, of which 1 were waited for; matrix products, arithmetic and copies ran while one was open for 0% of the time, Pallas kernels for 5%

profile of v5, /device:TPU:1, one launch (start us, length us, event | category | flops | bytes accessed | tf_op | source)
XLA Modules:
  0.0 75.0 jit_solution(16407787339877108405)
XLA Ops:
  0.6 0.0 copy-start.3
  0.6 0.0 copy-start.2
  0.7 0.9 %exponential_multiply_fusion.k_ref = f32[64,256]{1,0:T(8,128)S(1)} fusion(f32[64,256]{1,0:T(8,128)} %param.6, s32[64,256]{1,0:T(8,128)} %param.7), kind=kLoop, calls=%fused_computation | loop fusion | flops 65536 | bytes 196608 | tf_op jit(solution)/shard_map/mul | solution.py:32
  1.6 0.0 copy-start
  1.6 1.5 %copy-done = f32[30,64,256]{2,1,0:T(8,128)S(1)} copy-done((f32[30,64,256]{2,1,0:T(8,128)S(1)}, f32[30,64,256]{2,1,0:T(8,128)}, u32[]{:S(2)}) %copy-start) | copy-done | bytes 1966104
  3.1 0.0 copy-start.1
  3.2 0.8 %collective-permute-start.1 = (f32[64,256]{1,0:T(8,128)S(1)}, f32[64,256]{1,0:T(8,128)S(1)}, u32[]{:S(2)}, u32[]{:S(2)}) collective-permute-start(f32[64,256]{1,0:T(8,128)S(1)} %edges.1.edge_ref), channel_id=1, source_target_pairs={{8,16},{16,8},{24,32},{32,24},{40,48},{48,40},{56,64},{64,56},{72,... | collective-permute-start | bytes 196616 | tf_op jit(solution)/shard_map/ppermute | solution.py:645
  4.0 6.6 %collective-permute-start = (f32[64,256]{1,0:T(8,128)S(1)}, f32[64,256]{1,0:T(8,128)S(1)}, u32[]{:S(2)}, u32[]{:S(2)}) collective-permute-start(f32[64,256]{1,0:T(8,128)S(1)} %edges.1.edge_ref), channel_id=1, source_target_pairs={{0,8},{8,0},{16,24},{24,16},{32,40},{40,32},{48,56},{56,48},{64,72... | collective-permute-start | bytes 196616 | tf_op jit(solution)/shard_map/ppermute | solution.py:644
  10.6 0.0 copy-done.3
  10.6 0.0 copy-done.2
  10.6 0.0 copy-done.1
  10.6 3.7 %assemble.1 = (f32[32,128]{1,0:T(8,128)S(1)}, f32[32,128]{1,0:T(8,128)S(1)}) custom-call(f32[30,64,256]{2,1,0:T(8,128)S(1)} %copy-done.1, f32[64,256]{1,0:T(8,128)S(1)} %exponential_multiply_fusion.k_ref, f32[64,256]{1,0:T(8,128)S(1)} %copy-done.2, f32[64,256]{1,0:T(8,128)S(1)} %copy-done.3), custom_call_target="tpu_custom_call" | custom-call | flops 1610612736 | bytes 2097152 | tf_op jit(solution)/shard_map/assemble/pallas_call | solution.py:131
  14.3 0.1 pad_add_fusion.place_ref
  14.4 0.0 collective-permute-done.1.b_ref
  14.4 0.0 collective-permute-done.a_ref
  14.4 0.8 %rim.1 = f32[8,48,128]{2,1,0:T(8,128)S(1)} custom-call(s32[2]{0:T(128)S(1)} %pad_add_fusion.place_ref, f32[64,256]{1,0:T(8,128)S(1)} %edges.1.edge_ref, f32[64,256]{1,0:T(8,128)S(1)} %collective-permute-done.a_ref, f32[64,256]{1,0:T(8,128)S(1)} %collective-permute-done.1.b_ref, f32[32,128]{1,0:T(8,128)S(1)} %get-tuple-element.4.p_ref, ...), custom_call_target="tpu_custom_call" | custom-call | tf_op jit(solution)/shard_map/rim/pallas_call | solution.py:169
  15.2 11.2 %all_to_all.10.g_ref = f32[8,48,128]{2,1,0:T(8,128)S(1)} all-to-all(f32[8,48,128]{2,1,0:T(8,128)S(1)} %rim.1), channel_id=1, replica_groups=mesh['sub'=64,'own'=8] {'own'}, dimensions={0} | all-to-all | bytes 393216 | tf_op jit(solution)/shard_map/all_to_all | solution.py:648
  26.4 1.8 %total.1 = f32[64,8,128]{2,1,0:T(8,128)S(1)} custom-call(s32[2]{0:T(128)S(1)} %pad_add_fusion.place_ref, f32[8,48,128]{2,1,0:T(8,128)S(1)} %all_to_all.10.g_ref), custom_call_target="tpu_custom_call" | custom-call | tf_op jit(solution)/shard_map/total/pallas_call | solution.py:225
  28.3 26.8 %all_to_all.11.mine_ref = f32[64,8,128]{2,1,0:T(8,128)S(1)} all-to-all(f32[64,8,128]{2,1,0:T(8,128)S(1)} %total.1), channel_id=1, replica_groups=mesh['sub'=64,'own'=8] {'sub'}, dimensions={0} | all-to-all | bytes 524288 | tf_op jit(solution)/shard_map/all_to_all | solution.py:649
  55.1 5.5 %collective-permute-start.2 = (f32[64,8,128]{2,1,0:T(8,128)S(1)}, f32[64,8,128]{2,1,0:T(8,128)S(1)}, u32[]{:S(2)}, u32[]{:S(2)}) collective-permute-start(f32[64,8,128]{2,1,0:T(8,128)S(1)} %all_to_all.11.mine_ref), channel_id=1, source_target_pairs={{0,1},{1,0},{2,3},{3,2},{4,5},{5,4},{6,7},{7,6},{8,9},{9,8},{10,11... | collective-permute-start | bytes 786440 | tf_op jit(solution)/shard_map/ppermute | solution.py:650
  60.6 1.0 %collective-permute-done.2.other_ref = f32[64,8,128]{2,1,0:T(8,128)S(1)} collective-permute-done((f32[64,8,128]{2,1,0:T(8,128)S(1)}, f32[64,8,128]{2,1,0:T(8,128)S(1)}, u32[]{:S(2)}, u32[]{:S(2)}) %collective-permute-start.2) | collective-permute-done | bytes 262176 | tf_op jit(solution)/shard_map/ppermute | solution.py:650
  61.6 13.5 %solve.1 = (f32[1,30]{1,0:T(1,128)}, f32[64,256]{1,0:T(8,128)}) custom-call(s32[2]{0:T(128)S(1)} %pad_add_fusion.place_ref, f32[64,8,128]{2,1,0:T(8,128)S(1)} %all_to_all.11.mine_ref, f32[64,8,128]{2,1,0:T(8,128)S(1)} %collective-permute-done.2.other_ref, f32[30,64,256]{2,1,0:T(8,128)S(1)} %copy-done.1, f32[64,256]{1,0:T(8,128)S(1)} %exponential_multiply_fusion.k_ref, ...), custom_call_target="tpu_custom_call" | custom-call | tf_op jit(solution)/shard_map/solve/pallas_call | solution.py:626
  (1 shorter events, 0.0 us)
Async XLA Ops:
  0.6 9.9 %copy-start.3 = (f32[64,256]{1,0:T(8,128)S(1)}, f32[64,256]{1,0:T(8,128)}, u32[]{:S(2)}) copy-start(f32[64,256]{1,0:T(8,128)} %rs_ref.3) | copy-start | bytes 196612
  0.6 9.9 %copy-start.2 = (f32[64,256]{1,0:T(8,128)S(1)}, f32[64,256]{1,0:T(8,128)}, u32[]{:S(2)}) copy-start(f32[64,256]{1,0:T(8,128)} %st_ref.3) | copy-start | bytes 196612
  1.6 1.5 %copy-start = (f32[30,64,256]{2,1,0:T(8,128)S(1)}, f32[30,64,256]{2,1,0:T(8,128)}, u32[]{:S(2)}) copy-start(f32[30,64,256]{2,1,0:T(8,128)} %z_ref.5) | copy-start | bytes 5898244
  3.1 7.5 %copy-start.1 = (f32[30,64,256]{2,1,0:T(8,128)S(1)}, f32[30,64,256]{2,1,0:T(8,128)}, u32[]{:S(2)}) copy-start(f32[30,64,256]{2,1,0:T(8,128)} %z_ref.5) | copy-start | bytes 5898244
  3.2 11.2 %collective-permute-start.1 = (f32[64,256]{1,0:T(8,128)S(1)}, f32[64,256]{1,0:T(8,128)S(1)}, u32[]{:S(2)}, u32[]{:S(2)}) collective-permute-start(f32[64,256]{1,0:T(8,128)S(1)} %edges.1.edge_ref), channel_id=1, source_target_pairs={{8,16},{16,8},{24,32},{32,24},{40,48},{48,40},{56,64},{64,56},{72,... | collective-permute-start | bytes 196616 | tf_op jit(solution)/shard_map/ppermute | solution.py:645
  4.0 10.4 %collective-permute-start = (f32[64,256]{1,0:T(8,128)S(1)}, f32[64,256]{1,0:T(8,128)S(1)}, u32[]{:S(2)}, u32[]{:S(2)}) collective-permute-start(f32[64,256]{1,0:T(8,128)S(1)} %edges.1.edge_ref), channel_id=1, source_target_pairs={{0,8},{8,0},{16,24},{24,16},{32,40},{40,32},{48,56},{56,48},{64,72... | collective-permute-start | bytes 196616 | tf_op jit(solution)/shard_map/ppermute | solution.py:644
  55.1 6.5 %collective-permute-start.2 = (f32[64,8,128]{2,1,0:T(8,128)S(1)}, f32[64,8,128]{2,1,0:T(8,128)S(1)}, u32[]{:S(2)}, u32[]{:S(2)}) collective-permute-start(f32[64,8,128]{2,1,0:T(8,128)S(1)} %all_to_all.11.mine_ref), channel_id=1, source_target_pairs={{0,1},{1,0},{2,3},{3,2},{4,5},{5,4},{6,7},{7,6},{8,9},{9,8},{10,11... | collective-permute-start | bytes 786440 | tf_op jit(solution)/shard_map/ppermute | solution.py:650
